TPU v7x, 256 devices: a whole 4x4x8 slice. The times are simulated.
256 devices in a mesh: lon: 16 (over x, y_hi, core), lat: 16 (over z, y_lo).
Axes of the slice: x: 4, y: 4 (y_hi: 2, y_lo: 2; y = y_hi * 2 + y_lo), z: 8, core: 2. Of those that a mesh axis runs over, the one named last changes fastest.
Arguments:
- zonal_current: float32 [4, 512, 16384], P(None, 'lat', 'lon'), may hold values from -6 to 6
- meridian_current: float32 [4, 512, 16384], P(None, 'lat', 'lon'), may hold values from -6 to 6
- thermal_deviation: float32 [4, 512, 16384], P(None, 'lat', 'lon'), may hold values from -6 to 6
- saltiness_deviation: float32 [4, 512, 16384], P(None, 'lat', 'lon'), may hold values from -6 to 6
- dye_quantity: float32 [4, 512, 16384], P(None, 'lat', 'lon'), may hold values from -6 to 6
- water_indicator: int32 [4, 512, 16384], P(None, 'lat', 'lon'), may hold values from 0 to 1, as said below
Outputs:
- zonal_out: float32 [4, 512, 16384], P(None, 'lat', 'lon')
- meridional_out: float32 [4, 512, 16384], P(None, 'lat', 'lon')
- temperature_out: float32 [4, 512, 16384], P(None, 'lat', 'lon')
- salinity_out: float32 [4, 512, 16384], P(None, 'lat', 'lon')
- tracer_out: float32 [4, 512, 16384], P(None, 'lat', 'lon')
Inputs may be any that keep to these rules, and one draw needn't show every extreme that they name: `water_indicator`: A cell that is sea at some level is sea at every level above it.
All inputs are finite; a program needn't handle non-finite values.
Results may differ from a plain program's by a relative error of at most 0.00002.
Values sent between devices are 32-bit elements; how exact they have to be, the bound alone decides.
No kernel may reach another device: no remote copies, remote signals or barrier semaphores. Data moves between devices by JAX's collectives and lax.ppermute only.
A program may use at most 64 MiB of HBM per device.

v0:
```python
import jax
import jax.numpy as jnp
from jax import lax
from jax.sharding import PartitionSpec as P

ADVECTION = 0.25
DIFFUSION = 0.2
PRESSURE_GAIN = 0.3
EXPAND_T = 0.4
EXPAND_S = 0.6
CORIOLIS_BASE = 0.1
CORIOLIS_SLOPE = 0.4


def extended_2(block, sides, width, periodic):
    for axis, dim in sides:
        count = lax.axis_size(axis)
        forward = [(i, i + 1) for i in range(count - 1)]
        if periodic:
            forward.append((count - 1, 0))
        backward = [(target, source) for source, target in forward]
        low = lax.ppermute(
            lax.slice_in_dim(block, block.shape[dim] - width, None, axis=dim), axis, forward
        )
        high = lax.ppermute(lax.slice_in_dim(block, 0, width, axis=dim), axis, backward)
        block = jnp.concatenate([low, block, high], axis=dim)
    return block


def from_partner(block, axis, apart):
    count = lax.axis_size(axis)
    route = []
    for low in range(count):
        high = low | 1 << apart
        if high != low and high < count:
            route += [(low, high), (high, low)]
    return lax.ppermute(block, axis, route)


def coriolis(row_index, total_rows):
    mirrored = jnp.minimum(row_index, 2 * total_rows - 1 - row_index)
    return CORIOLIS_BASE + CORIOLIS_SLOPE * (mirrored.astype(jnp.float32) + 0.5) / total_rows


def advance(prognostic_bundle, sea, coriolis_rows):
    zonal = prognostic_bundle[0]
    meridional = prognostic_bundle[1]
    face_x = sea[:, 1:-1, 1:] * sea[:, 1:-1, :-1]
    face_y = sea[:, 1:, 1:-1] * sea[:, :-1, 1:-1]
    speed_x = 0.5 * (zonal[:, 1:-1, 1:] + zonal[:, 1:-1, :-1])
    speed_y = 0.5 * (meridional[:, 1:, 1:-1] + meridional[:, :-1, 1:-1])
    east_side = prognostic_bundle[:, :, 1:-1, 1:]
    west_side = prognostic_bundle[:, :, 1:-1, :-1]
    north_side = prognostic_bundle[:, :, 1:, 1:-1]
    south_side = prognostic_bundle[:, :, :-1, 1:-1]
    flux_x = face_x * (
        ADVECTION * speed_x * (0.5 * (east_side + west_side)) - DIFFUSION * (east_side - west_side)
    )
    flux_y = face_y * (
        ADVECTION * speed_y * (0.5 * (north_side + south_side))
        - DIFFUSION * (north_side - south_side)
    )
    tendency = -(flux_x[..., 1:] - flux_x[..., :-1] + (flux_y[..., 1:, :] - flux_y[..., :-1, :]))
    density = EXPAND_S * prognostic_bundle[3] - EXPAND_T * prognostic_bundle[2]
    pressure = jnp.cumsum(density, axis=0) - 0.5 * density
    grad_x = 0.5 * (
        face_x[:, :, 1:] * (pressure[:, 1:-1, 2:] - pressure[:, 1:-1, 1:-1])
        + face_x[:, :, :-1] * (pressure[:, 1:-1, 1:-1] - pressure[:, 1:-1, :-2])
    )
    grad_y = 0.5 * (
        face_y[:, 1:, :] * (pressure[:, 2:, 1:-1] - pressure[:, 1:-1, 1:-1])
        + face_y[:, :-1, :] * (pressure[:, 1:-1, 1:-1] - pressure[:, :-2, 1:-1])
    )
    centre = prognostic_bundle[:, :, 1:-1, 1:-1]
    spin = coriolis_rows[None, :, None]
    tend_u = tendency[0] + spin * centre[1] - PRESSURE_GAIN * grad_x
    tend_v = tendency[1] - spin * centre[0] - PRESSURE_GAIN * grad_y
    tendency = jnp.concatenate([tend_u[None], tend_v[None], tendency[2:]], axis=0)
    return sea[None, :, 1:-1, 1:-1] * (centre + tendency)


def extend_rims(stacked_levels, flip_signs, width):
    columns = extended_2(stacked_levels, (("lon", 2),), width, True)
    height = columns.shape[1]
    fold_strip = columns[:, height - width :, :][:, ::-1, ::-1] * flip_signs
    for bit_index in range(lax.axis_size("lon").bit_length() - 1):
        fold_strip = from_partner(fold_strip, "lon", bit_index)
    framed = extended_2(columns, (("lat", 1),), width, False)
    top_device = lax.axis_index("lat") == lax.axis_size("lat") - 1
    upper_rows = jnp.where(top_device, fold_strip, framed[:, height + width :, :])
    return jnp.concatenate([framed[:, : height + width, :], upper_rows], axis=1)


def per_device(
    zonal_current,
    meridian_current,
    thermal_deviation,
    saltiness_deviation,
    dye_quantity,
    water_indicator,
):
    level_count, height, breadth = zonal_current.shape
    field_rows = 5 * level_count
    flip_signs = jnp.repeat(jnp.array([-1.0, -1.0, 1.0, 1.0, 1.0, 1.0], jnp.float32), level_count)[
        :, None, None
    ]
    stacked_levels = jnp.concatenate(
        [
            zonal_current,
            meridian_current,
            thermal_deviation,
            saltiness_deviation,
            dye_quantity,
            water_indicator.astype(jnp.float32),
        ],
        axis=0,
    )
    total_rows = height * lax.axis_size("lat")
    first_row = lax.axis_index("lat") * height
    extended = extend_rims(stacked_levels, flip_signs, 1)
    sea = extended[field_rows:]
    coriolis_rows = coriolis(first_row + jnp.arange(height, dtype=jnp.int32), total_rows)
    prognostic_bundle = advance(
        extended[:field_rows].reshape(5, level_count, height + 2, breadth + 2), sea, coriolis_rows
    )
    extended = extend_rims(
        prognostic_bundle.reshape(field_rows, height, breadth), flip_signs[:field_rows], 1
    )
    prognostic_bundle = advance(
        extended.reshape(5, level_count, height + 2, breadth + 2), sea, coriolis_rows
    )
    return (
        prognostic_bundle[0],
        prognostic_bundle[1],
        prognostic_bundle[2],
        prognostic_bundle[3],
        prognostic_bundle[4],
    )


def solution(mesh):
    return jax.shard_map(
        per_device,
        mesh=mesh,
        in_specs=(
            P(None, "lat", "lon"),
            P(None, "lat", "lon"),
            P(None, "lat", "lon"),
            P(None, "lat", "lon"),
            P(None, "lat", "lon"),
            P(None, "lat", "lon"),
        ),
        out_specs=(
            P(None, "lat", "lon"),
            P(None, "lat", "lon"),
            P(None, "lat", "lon"),
            P(None, "lat", "lon"),
            P(None, "lat", "lon"),
        ),
        check_vma=False,
    )
```

profile of v0, /device:TPU:104, one launch (start us, length us, event | category | flops | bytes accessed | tf_op | source)
XLA Modules:
  0.0 121.8 jit_solution(15591274697098989534)
XLA Ops:
  0.7 1.2 constant_dynamic-update-slice_fusion.5
  1.9 1.1 constant_dynamic-update-slice_fusion.4
  3.0 1.1 constant_dynamic-update-slice_fusion.3
  4.2 1.6 %copy-done.5 = f32[24,32,1024]{2,1,0:T(8,128)} copy-done((f32[24,32,1024]{2,1,0:T(8,128)}, f32[24,32,1024]{2,1,0:T(8,128)S(1)}, u32[]{:S(2)}) %copy-start.5) | copy-done | bytes 3145752
  5.9 0.2 fusion.64
  6.1 4.0 %collective-permute-start.1 = (f32[24,32,1]{2,1,0:T(8,128)S(1)}, f32[24,32,1]{2,1,0:T(8,128)S(1)}, u32[]{:S(2)}, u32[]{:S(2)}) collective-permute-start(f32[24,32,1]{2,1,0:T(8,128)S(1)} %get-tuple-element.15), channel_id=1, source_target_pairs={{16,0},{32,16},{48,32},{64,48},{80,64},{96,80},{112,96},{128,112},... | collective-permute-start | bytes 9224 | tf_op jit(solution)/shard_map/ppermute | solution.py:25
  10.2 5.2 %collective-permute-done.1 = f32[24,32,1]{2,1,0:T(8,128)S(1)} collective-permute-done((f32[24,32,1]{2,1,0:T(8,128)S(1)}, f32[24,32,1]{2,1,0:T(8,128)S(1)}, u32[]{:S(2)}, u32[]{:S(2)}) %collective-permute-start.1) | collective-permute-done | bytes 3104 | tf_op jit(solution)/shard_map/ppermute | solution.py:25
  15.4 0.7 copy-done.8
  16.1 4.8 %collective-permute-done = f32[24,32,1]{2,1,0:T(8,128)} collective-permute-done((f32[24,32,1]{2,1,0:T(8,128)S(1)}, f32[24,32,1]{2,1,0:T(8,128)}, u32[]{:S(2)}, u32[]{:S(2)}) %collective-permute-start) | collective-permute-done | bytes 3104 | tf_op jit(solution)/shard_map/ppermute | solution.py:22
  21.0 3.8 %concatenate.50 = f32[24,32,1026]{2,1,0:T(8,128)S(1)} concatenate(f32[24,32,1]{2,1,0:T(8,128)} %collective-permute-done, f32[24,32,1024]{2,1,0:T(8,128)} %copy-done.5, f32[24,32,1]{2,1,0:T(8,128)} %copy-done.8), dimensions={2} | concatenate | bytes 6303744 | tf_op jit(solution)/shard_map/concatenate | solution.py:26
  24.8 0.8 fusion.63
  25.7 5.2 %reverse = f32[24,1,1152]{2,1,0:T(1,128)} reverse(f32[24,1,1152]{2,1,0:T(1,128)} %bitcast.88), dimensions={1,2} | reverse | bytes 221184
  30.9 1.2 broadcast_multiply_fusion
  32.1 0.1 collective-permute-start.3
  32.2 1.4 %collective-permute-done.3 = f32[24,1,1026]{2,1,0:T(1,128)} collective-permute-done((f32[24,1,1026]{2,1,0:T(1,128)S(1)}, f32[24,1,1026]{2,1,0:T(1,128)}, u32[]{:S(2)}, u32[]{:S(2)}) %collective-permute-start.3) | collective-permute-done | bytes 98528 | tf_op jit(solution)/shard_map/ppermute | solution.py:37
  33.6 1.1 collective-permute-start.4
  34.8 1.9 %convert_element_type.10 = f32[4,32,1024]{2,1,0:T(8,128)} convert(s32[4,32,1024]{2,1,0:T(8,128)} %param.12) | non-fusion elementwise | flops 131072 | bytes 1048576 | tf_op jit(solution)/shard_map/convert_element_type | solution.py:114
  36.7 3.9 %collective-permute-done.4 = f32[24,1,1026]{2,1,0:T(1,128)} collective-permute-done((f32[24,1,1026]{2,1,0:T(1,128)}, f32[24,1,1026]{2,1,0:T(1,128)}, u32[]{:S(2)}, u32[]{:S(2)}) %collective-permute-start.4) | collective-permute-done | bytes 98528 | tf_op jit(solution)/shard_map/ppermute | solution.py:37
  40.6 5.8 %collective-permute-start.2 = (f32[24,1,1026]{2,1,0:T(1,128)}, f32[24,1,1026]{2,1,0:T(1,128)S(1)}, u32[]{:S(2)}, u32[]{:S(2)}) collective-permute-start(f32[24,1,1026]{2,1,0:T(1,128)} %get-tuple-element.14), channel_id=1, source_target_pairs={{0,1},{1,2},{2,3},{3,4},{4,5},{5,6},{6,7},{7,8},{8,9},{9,10},{10,1... | collective-permute-start | bytes 295496 | tf_op jit(solution)/shard_map/ppermute | solution.py:22
  46.4 1.9 %collective-permute-start.7 = (f32[24,1,1026]{2,1,0:T(1,128)}, f32[24,1,1026]{2,1,0:T(1,128)S(1)}, u32[]{:S(2)}, u32[]{:S(2)}) collective-permute-start(f32[24,1,1026]{2,1,0:T(1,128)} %get-tuple-element.13), channel_id=1, source_target_pairs={{1,0},{2,1},{3,2},{4,3},{5,4},{6,5},{7,6},{8,7},{9,8},{10,9},{11,1... | collective-permute-start | bytes 295496 | tf_op jit(solution)/shard_map/ppermute | solution.py:25
  48.4 2.3 %collective-permute-start.6 = (f32[24,1,1026]{2,1,0:T(1,128)S(1)}, f32[24,1,1026]{2,1,0:T(1,128)S(1)}, u32[]{:S(2)}, u32[]{:S(2)}) collective-permute-start(f32[24,1,1026]{2,1,0:T(1,128)S(1)} %collective-permute-done.5), channel_id=1, source_target_pairs={{0,128},{128,0},{16,144},{144,16},{32,160},{160,32},{48,176},{176,... | collective-permute-start | bytes 295496 | tf_op jit(solution)/shard_map/ppermute | solution.py:37
  50.7 1.9 %maximum_multiply_fusion.3 = (f32[4,32,1025]{2,1,0:T(8,128)S(1)}, f32[4,32,1025]{2,1,0:T(8,128)S(1)}) fusion(f32[24,32,1024]{2,1,0:T(8,128)} %copy-done.5, f32[24,32,1]{2,1,0:T(8,128)} %collective-permute-done, f32[24,32,1]{2,1,0:T(8,128)} %copy-done.8), kind=kLoop, calls=%fused_computation.43 | loop fusion | flops 918400 | bytes 4201472 | tf_op jit(solution)/shard_map/mul | solution.py:48
  52.6 2.8 %collective-permute-done.7 = f32[24,1,1026]{2,1,0:T(1,128)S(1)} collective-permute-done((f32[24,1,1026]{2,1,0:T(1,128)}, f32[24,1,1026]{2,1,0:T(1,128)S(1)}, u32[]{:S(2)}, u32[]{:S(2)}) %collective-permute-start.7) | collective-permute-done | bytes 98528 | tf_op jit(solution)/shard_map/ppermute | solution.py:25
  55.4 0.5 pad_maximum_fusion
  55.9 0.2 slice.370
  56.2 1.4 %subtract_multiply_fusion.3 = f32[5,4,32,1025]{3,2,1,0:T(8,128)S(1)} fusion(f32[5,4,34,1026]{3,2,1,0:T(8,128)S(1)} %bitcast.78, f32[4,32,1025]{2,1,0:T(8,128)S(1)} %get-tuple-element.10, f32[4,32,1025]{2,1,0:T(8,128)S(1)} %get-tuple-element.9), kind=kLoop, calls=%fused_computation.5 | loop fusion | flops 3936000 | bytes 8921600 | tf_op jit(solution)/shard_map/mul | solution.py:56
  57.6 0.8 maximum_multiply_fusion.2
  58.4 1.8 %subtract_multiply_fusion.1 = f32[5,4,33,1024]{3,2,1,0:T(8,128)S(1)} fusion(f32[5,4,34,1026]{3,2,1,0:T(8,128)S(1)} %bitcast.79, f32[4,33,1024]{2,1,0:T(8,128)S(1)} %get-tuple-element.12, f32[4,33,1024]{2,1,0:T(8,128)S(1)} %get-tuple-element.11), kind=kLoop, calls=%fused_computation.3 | loop fusion | flops 4055040 | bytes 9191424 | tf_op jit(solution)/shard_map/mul | solution.py:59
  60.2 0.9 fusion.4
  61.1 0.2 slice.393
  61.3 0.9 reduce-window_subtract_fusion.1
  62.2 1.1 fusion.46
  63.3 1.0 fusion.5
  64.3 0.9 fusion.66
  65.3 0.2 collective-permute-start.9
  65.5 0.3 collective-permute-start.8
  65.9 4.5 %collective-permute-done.9 = f32[20,32,1]{2,1,0:T(8,128)S(1)} collective-permute-done((f32[20,32,1]{2,1,0:T(8,128)}, f32[20,32,1]{2,1,0:T(8,128)S(1)}, u32[]{:S(2)}, u32[]{:S(2)}) %collective-permute-start.9) | collective-permute-done | bytes 2592 | tf_op jit(solution)/shard_map/ppermute | solution.py:25
  70.4 5.5 %collective-permute-done.8 = f32[20,32,1]{2,1,0:T(8,128)} collective-permute-done((f32[20,32,1]{2,1,0:T(8,128)}, f32[20,32,1]{2,1,0:T(8,128)}, u32[]{:S(2)}, u32[]{:S(2)}) %collective-permute-start.8) | collective-permute-done | bytes 2592 | tf_op jit(solution)/shard_map/ppermute | solution.py:22
  75.9 4.1 %concatenate.57 = f32[20,32,1026]{2,1,0:T(8,128)} concatenate(f32[20,32,1]{2,1,0:T(8,128)} %collective-permute-done.8, f32[20,32,1024]{2,1,0:T(8,128)S(1)} %bitcast.83, f32[20,32,1]{2,1,0:T(8,128)S(1)} %collective-permute-done.9), dimensions={2} | concatenate | bytes 5253120 | tf_op jit(solution)/shard_map/concatenate | solution.py:26
  79.9 2.1 %fusion.65 = (f32[20,1,1026]{2,1,0:T(1,128)}, f32[20,1,1026]{2,1,0:T(1,128)}) fusion(f32[20,32,1026]{2,1,0:T(8,128)} %concatenate.57), kind=kLoop, calls=%fused_computation.123 | loop fusion | bytes 328320 | tf_op jit(solution)/shard_map/slice | solution.py:25
  82.1 5.1 %reverse.1 = f32[20,1,1152]{2,1,0:T(1,128)} reverse(f32[20,1,1152]{2,1,0:T(1,128)} %bitcast.89), dimensions={1,2} | reverse | bytes 184320
  87.2 1.3 %broadcast_multiply_fusion.1 = f32[20,1,1026]{2,1,0:T(1,128)S(1)} fusion(f32[20]{0:T(128)S(1)} %mul.265, f32[20,1,1152]{2,1,0:T(1,128)} %reverse.1), kind=kLoop, calls=%fused_computation.104 | loop fusion | flops 20520 | bytes 164240 | tf_op jit(solution)/shard_map/mul | solution.py:85
  88.7 1.3 %collective-permute-done.11 = f32[20,1,1026]{2,1,0:T(1,128)S(1)} collective-permute-done((f32[20,1,1026]{2,1,0:T(1,128)S(1)}, f32[20,1,1026]{2,1,0:T(1,128)S(1)}, u32[]{:S(2)}, u32[]{:S(2)}) %collective-permute-start.11) | collective-permute-done | bytes 82112 | tf_op jit(solution)/shard_map/ppermute | solution.py:37
  89.9 2.7 %collective-permute-start.12 = (f32[20,1,1026]{2,1,0:T(1,128)S(1)}, f32[20,1,1026]{2,1,0:T(1,128)S(1)}, u32[]{:S(2)}, u32[]{:S(2)}) collective-permute-start(f32[20,1,1026]{2,1,0:T(1,128)S(1)} %collective-permute-done.11), channel_id=1, source_target_pairs={{0,32},{32,0},{16,48},{48,16},{64,96},{96,64},{80,112},{112,80},{1... | collective-permute-start | bytes 246248 | tf_op jit(solution)/shard_map/ppermute | solution.py:37
  92.6 3.6 %collective-permute-done.12 = f32[20,1,1026]{2,1,0:T(1,128)S(1)} collective-permute-done((f32[20,1,1026]{2,1,0:T(1,128)S(1)}, f32[20,1,1026]{2,1,0:T(1,128)S(1)}, u32[]{:S(2)}, u32[]{:S(2)}) %collective-permute-start.12) | collective-permute-done | bytes 82112 | tf_op jit(solution)/shard_map/ppermute | solution.py:37
  96.2 0.7 collective-permute-start.13
  96.9 5.5 %collective-permute-start.10 = (f32[20,1,1026]{2,1,0:T(1,128)}, f32[20,1,1026]{2,1,0:T(1,128)S(1)}, u32[]{:S(2)}, u32[]{:S(2)}) collective-permute-start(f32[20,1,1026]{2,1,0:T(1,128)} %get-tuple-element.18), channel_id=1, source_target_pairs={{0,1},{1,2},{2,3},{3,4},{4,5},{5,6},{6,7},{7,8},{8,9},{9,10},{10,1... | collective-permute-start | bytes 246248 | tf_op jit(solution)/shard_map/ppermute | solution.py:22
  102.4 1.9 %collective-permute-start.15 = (f32[20,1,1026]{2,1,0:T(1,128)}, f32[20,1,1026]{2,1,0:T(1,128)S(1)}, u32[]{:S(2)}, u32[]{:S(2)}) collective-permute-start(f32[20,1,1026]{2,1,0:T(1,128)} %get-tuple-element.17), channel_id=1, source_target_pairs={{1,0},{2,1},{3,2},{4,3},{5,4},{6,5},{7,6},{8,7},{9,8},{10,9},{11,1... | collective-permute-start | bytes 246248 | tf_op jit(solution)/shard_map/ppermute | solution.py:25
  104.3 2.8 %collective-permute-start.14 = (f32[20,1,1026]{2,1,0:T(1,128)S(1)}, f32[20,1,1026]{2,1,0:T(1,128)S(1)}, u32[]{:S(2)}, u32[]{:S(2)}) collective-permute-start(f32[20,1,1026]{2,1,0:T(1,128)S(1)} %collective-permute-done.13), channel_id=1, source_target_pairs={{0,128},{128,0},{16,144},{144,16},{32,160},{160,32},{48,176},{176,... | collective-permute-start | bytes 246248 | tf_op jit(solution)/shard_map/ppermute | solution.py:37
  107.1 1.1 fusion.15
  108.2 3.0 %collective-permute-done.15 = f32[20,1,1026]{2,1,0:T(1,128)S(1)} collective-permute-done((f32[20,1,1026]{2,1,0:T(1,128)}, f32[20,1,1026]{2,1,0:T(1,128)S(1)}, u32[]{:S(2)}, u32[]{:S(2)}) %collective-permute-start.15) | collective-permute-done | bytes 82112 | tf_op jit(solution)/shard_map/ppermute | solution.py:25
  111.2 0.1 broadcast_select_fusion.1
  111.3 0.4 pad_maximum_fusion.1
  111.7 0.4 reduce-window_subtract_fusion
  112.1 0.7 copy-done.2
  112.8 1.4 %subtract_multiply_fusion.2 = f32[5,4,32,1025]{3,2,1,0:T(8,128)S(1)} fusion(f32[5,4,34,1026]{3,2,1,0:T(8,128)S(1)} %bitcast.74, f32[4,32,1025]{2,1,0:T(8,128)S(1)} %fusion.15, f32[4,32,1025]{2,1,0:T(8,128)S(1)} %copy-done.2), kind=kLoop, calls=%fused_computation.4 | loop fusion | flops 3936000 | bytes 8921600 | tf_op jit(solution)/shard_map/mul | solution.py:56
  114.2 0.4 fusion.11
  114.7 0.6 copy-done.4
  115.3 1.9 %subtract_multiply_fusion = f32[5,4,33,1024]{3,2,1,0:T(8,128)S(1)} fusion(f32[5,4,34,1026]{3,2,1,0:T(8,128)S(1)} %bitcast.75, f32[4,33,1024]{2,1,0:T(8,128)S(1)} %fusion.11, f32[4,33,1024]{2,1,0:T(8,128)S(1)} %copy-done.4), kind=kLoop, calls=%fused_computation.2 | loop fusion | flops 4055040 | bytes 9191424 | tf_op jit(solution)/shard_map/mul | solution.py:59
  117.2 0.9 fusion.1
  118.1 0.1 slice.418
  118.2 1.1 fusion.30
  119.2 1.0 fusion.2
  120.3 1.5 %slice_bitcast_fusion = (f32[4,32,1024]{2,1,0:T(8,128)}, f32[4,32,1024]{2,1,0:T(8,128)}, f32[4,32,1024]{2,1,0:T(8,128)}, f32[4,32,1024]{2,1,0:T(8,128)}, f32[4,32,1024]{2,1,0:T(8,128)}) fusion(f32[5,4,32,1024]{3,2,1,0:T(8,128)S(1)} %fusion.2), kind=kLoop, calls=%fused_computation.44 | loop fusion | bytes 5242880 | tf_op jit(solution)/shard_map/squeeze | solution.py:137
  (40 shorter events, 0.6 us)
Async XLA Ops:
  0.6 3.4 %copy-start.9 = (f32[4,32,1024]{2,1,0:T(8,128)S(1)}, f32[4,32,1024]{2,1,0:T(8,128)}, u32[]{:S(2)}) copy-start(f32[4,32,1024]{2,1,0:T(8,128)} %param.10) | copy-start | bytes 1572868
  0.6 3.5 %copy-start.10 = (f32[4,32,1024]{2,1,0:T(8,128)S(1)}, f32[4,32,1024]{2,1,0:T(8,128)}, u32[]{:S(2)}) copy-start(f32[4,32,1024]{2,1,0:T(8,128)} %param.11) | copy-start | bytes 1572868
  0.7 3.5 %copy-start.7 = (s32[4,32,1024]{2,1,0:T(8,128)S(1)}, s32[4,32,1024]{2,1,0:T(8,128)}, u32[]{:S(2)}) copy-start(s32[4,32,1024]{2,1,0:T(8,128)} %param.12) | copy-start | bytes 1572868
  2.9 7.1 %copy-start.12 = (f32[6]{0:T(128)S(1)}, f32[6]{0:T(128)}, u32[]{:S(2)}) copy-start(f32[6]{0:T(128)} %constant.56.clone) | copy-start | bytes 76
  4.2 1.6 %copy-start.5 = (f32[24,32,1024]{2,1,0:T(8,128)}, f32[24,32,1024]{2,1,0:T(8,128)S(1)}, u32[]{:S(2)}) copy-start(f32[24,32,1024]{2,1,0:T(8,128)S(1)} %constant_dynamic-update-slice_fusion) | copy-start | bytes 9437188
  6.1 9.3 %collective-permute-start.1 = (f32[24,32,1]{2,1,0:T(8,128)S(1)}, f32[24,32,1]{2,1,0:T(8,128)S(1)}, u32[]{:S(2)}, u32[]{:S(2)}) collective-permute-start(f32[24,32,1]{2,1,0:T(8,128)S(1)} %get-tuple-element.15), channel_id=1, source_target_pairs={{16,0},{32,16},{48,32},{64,48},{80,64},{96,80},{112,96},{128,112},... | collective-permute-start | bytes 9224 | tf_op jit(solution)/shard_map/ppermute | solution.py:25
  10.1 10.9 %collective-permute-start = (f32[24,32,1]{2,1,0:T(8,128)S(1)}, f32[24,32,1]{2,1,0:T(8,128)}, u32[]{:S(2)}, u32[]{:S(2)}) collective-permute-start(f32[24,32,1]{2,1,0:T(8,128)S(1)} %get-tuple-element.16), channel_id=1, source_target_pairs={{0,16},{16,32},{32,48},{48,64},{64,80},{80,96},{96,112},{112,128},... | collective-permute-start | bytes 9224 | tf_op jit(solution)/shard_map/ppermute | solution.py:22
  15.4 0.7 copy-start.8
  32.1 1.5 %collective-permute-start.3 = (f32[24,1,1026]{2,1,0:T(1,128)S(1)}, f32[24,1,1026]{2,1,0:T(1,128)}, u32[]{:S(2)}, u32[]{:S(2)}) collective-permute-start(f32[24,1,1026]{2,1,0:T(1,128)S(1)} %broadcast_multiply_fusion), channel_id=1, source_target_pairs={{0,16},{16,0},{32,48},{48,32},{64,80},{80,64},{96,112},{112,96},{1... | collective-permute-start | bytes 295496 | tf_op jit(solution)/shard_map/ppermute | solution.py:37
  33.6 6.9 %collective-permute-start.4 = (f32[24,1,1026]{2,1,0:T(1,128)}, f32[24,1,1026]{2,1,0:T(1,128)}, u32[]{:S(2)}, u32[]{:S(2)}) collective-permute-start(f32[24,1,1026]{2,1,0:T(1,128)} %collective-permute-done.3), channel_id=1, source_target_pairs={{0,32},{32,0},{16,48},{48,16},{64,96},{96,64},{80,112},{112,80},{1... | collective-permute-start | bytes 295496 | tf_op jit(solution)/shard_map/ppermute | solution.py:37
  40.6 7.8 %collective-permute-start.5 = (f32[24,1,1026]{2,1,0:T(1,128)}, f32[24,1,1026]{2,1,0:T(1,128)S(1)}, u32[]{:S(2)}, u32[]{:S(2)}) collective-permute-start(f32[24,1,1026]{2,1,0:T(1,128)} %collective-permute-done.4), channel_id=1, source_target_pairs={{0,64},{64,0},{16,80},{80,16},{32,96},{96,32},{48,112},{112,48},{1... | collective-permute-start | bytes 295496 | tf_op jit(solution)/shard_map/ppermute | solution.py:37
  40.6 14.8 %collective-permute-start.2 = (f32[24,1,1026]{2,1,0:T(1,128)}, f32[24,1,1026]{2,1,0:T(1,128)S(1)}, u32[]{:S(2)}, u32[]{:S(2)}) collective-permute-start(f32[24,1,1026]{2,1,0:T(1,128)} %get-tuple-element.14), channel_id=1, source_target_pairs={{0,1},{1,2},{2,3},{3,4},{4,5},{5,6},{6,7},{7,8},{8,9},{9,10},{10,1... | collective-permute-start | bytes 295496 | tf_op jit(solution)/shard_map/ppermute | solution.py:22
  46.4 9.0 %collective-permute-start.7 = (f32[24,1,1026]{2,1,0:T(1,128)}, f32[24,1,1026]{2,1,0:T(1,128)S(1)}, u32[]{:S(2)}, u32[]{:S(2)}) collective-permute-start(f32[24,1,1026]{2,1,0:T(1,128)} %get-tuple-element.13), channel_id=1, source_target_pairs={{1,0},{2,1},{3,2},{4,3},{5,4},{6,5},{7,6},{8,7},{9,8},{10,9},{11,1... | collective-permute-start | bytes 295496 | tf_op jit(solution)/shard_map/ppermute | solution.py:25
  48.4 7.0 %collective-permute-start.6 = (f32[24,1,1026]{2,1,0:T(1,128)S(1)}, f32[24,1,1026]{2,1,0:T(1,128)S(1)}, u32[]{:S(2)}, u32[]{:S(2)}) collective-permute-start(f32[24,1,1026]{2,1,0:T(1,128)S(1)} %collective-permute-done.5), channel_id=1, source_target_pairs={{0,128},{128,0},{16,144},{144,16},{32,160},{160,32},{48,176},{176,... | collective-permute-start | bytes 295496 | tf_op jit(solution)/shard_map/ppermute | solution.py:37
  52.6 9.6 %copy-start.1 = (f32[4,32,1025]{2,1,0:T(8,128)}, f32[4,32,1025]{2,1,0:T(8,128)S(1)}, u32[]{:S(2)}) copy-start(f32[4,32,1025]{2,1,0:T(8,128)S(1)} %get-tuple-element.9) | copy-start | bytes 1574404
  58.4 3.8 %copy-start.3 = (f32[4,33,1024]{2,1,0:T(8,128)}, f32[4,33,1024]{2,1,0:T(8,128)S(1)}, u32[]{:S(2)}) copy-start(f32[4,33,1024]{2,1,0:T(8,128)S(1)} %get-tuple-element.11) | copy-start | bytes 1622020
  62.2 1.1 copy-start.6
  63.3 2.5 %copy-start.11 = (f32[5]{0:T(128)S(1)}, f32[5]{0:T(128)}, u32[]{:S(2)}) copy-start(f32[5]{0:T(128)} %constant.57) | copy-start | bytes 64
  65.3 5.1 %collective-permute-start.9 = (f32[20,32,1]{2,1,0:T(8,128)}, f32[20,32,1]{2,1,0:T(8,128)S(1)}, u32[]{:S(2)}, u32[]{:S(2)}) collective-permute-start(f32[20,32,1]{2,1,0:T(8,128)} %get-tuple-element.24), channel_id=1, source_target_pairs={{16,0},{32,16},{48,32},{64,48},{80,64},{96,80},{112,96},{128,112},... | collective-permute-start | bytes 7688 | tf_op jit(solution)/shard_map/ppermute | solution.py:25
  65.5 10.4 %collective-permute-start.8 = (f32[20,32,1]{2,1,0:T(8,128)}, f32[20,32,1]{2,1,0:T(8,128)}, u32[]{:S(2)}, u32[]{:S(2)}) collective-permute-start(f32[20,32,1]{2,1,0:T(8,128)} %get-tuple-element.25), channel_id=1, source_target_pairs={{0,16},{16,32},{32,48},{48,64},{64,80},{80,96},{96,112},{112,128},... | collective-permute-start | bytes 7688 | tf_op jit(solution)/shard_map/ppermute | solution.py:22
  87.2 24.1 %copy-start = (f32[20,32,1026]{2,1,0:T(8,128)S(1)}, f32[20,32,1026]{2,1,0:T(8,128)}, u32[]{:S(2)}) copy-start(f32[20,32,1026]{2,1,0:T(8,128)} %concatenate.57) | copy-start | bytes 7879684
  88.6 1.4 %collective-permute-start.11 = (f32[20,1,1026]{2,1,0:T(1,128)S(1)}, f32[20,1,1026]{2,1,0:T(1,128)S(1)}, u32[]{:S(2)}, u32[]{:S(2)}) collective-permute-start(f32[20,1,1026]{2,1,0:T(1,128)S(1)} %broadcast_multiply_fusion.1), channel_id=1, source_target_pairs={{0,16},{16,0},{32,48},{48,32},{64,80},{80,64},{96,112},{112,96},{1... | collective-permute-start | bytes 246248 | tf_op jit(solution)/shard_map/ppermute | solution.py:37
  89.9 6.2 %collective-permute-start.12 = (f32[20,1,1026]{2,1,0:T(1,128)S(1)}, f32[20,1,1026]{2,1,0:T(1,128)S(1)}, u32[]{:S(2)}, u32[]{:S(2)}) collective-permute-start(f32[20,1,1026]{2,1,0:T(1,128)S(1)} %collective-permute-done.11), channel_id=1, source_target_pairs={{0,32},{32,0},{16,48},{48,16},{64,96},{96,64},{80,112},{112,80},{1... | collective-permute-start | bytes 246248 | tf_op jit(solution)/shard_map/ppermute | solution.py:37
  96.2 8.2 %collective-permute-start.13 = (f32[20,1,1026]{2,1,0:T(1,128)S(1)}, f32[20,1,1026]{2,1,0:T(1,128)S(1)}, u32[]{:S(2)}, u32[]{:S(2)}) collective-permute-start(f32[20,1,1026]{2,1,0:T(1,128)S(1)} %collective-permute-done.12), channel_id=1, source_target_pairs={{0,64},{64,0},{16,80},{80,16},{32,96},{96,32},{48,112},{112,48},{1... | collective-permute-start | bytes 246248 | tf_op jit(solution)/shard_map/ppermute | solution.py:37
  96.9 14.4 %collective-permute-start.10 = (f32[20,1,1026]{2,1,0:T(1,128)}, f32[20,1,1026]{2,1,0:T(1,128)S(1)}, u32[]{:S(2)}, u32[]{:S(2)}) collective-permute-start(f32[20,1,1026]{2,1,0:T(1,128)} %get-tuple-element.18), channel_id=1, source_target_pairs={{0,1},{1,2},{2,3},{3,4},{4,5},{5,6},{6,7},{7,8},{8,9},{9,10},{10,1... | collective-permute-start | bytes 246248 | tf_op jit(solution)/shard_map/ppermute | solution.py:22
  102.4 8.8 %collective-permute-start.15 = (f32[20,1,1026]{2,1,0:T(1,128)}, f32[20,1,1026]{2,1,0:T(1,128)S(1)}, u32[]{:S(2)}, u32[]{:S(2)}) collective-permute-start(f32[20,1,1026]{2,1,0:T(1,128)} %get-tuple-element.17), channel_id=1, source_target_pairs={{1,0},{2,1},{3,2},{4,3},{5,4},{6,5},{7,6},{8,7},{9,8},{10,9},{11,1... | collective-permute-start | bytes 246248 | tf_op jit(solution)/shard_map/ppermute | solution.py:25
  104.3 6.8 %collective-permute-start.14 = (f32[20,1,1026]{2,1,0:T(1,128)S(1)}, f32[20,1,1026]{2,1,0:T(1,128)S(1)}, u32[]{:S(2)}, u32[]{:S(2)}) collective-permute-start(f32[20,1,1026]{2,1,0:T(1,128)S(1)} %collective-permute-done.13), channel_id=1, source_target_pairs={{0,128},{128,0},{16,144},{144,16},{32,160},{160,32},{48,176},{176,... | collective-permute-start | bytes 246248 | tf_op jit(solution)/shard_map/ppermute | solution.py:37
  111.7 1.1 copy-start.2
  114.2 1.1 copy-start.4
where the time goes:
time: 124 us; the launch traced here: 122 us
  waiting for transfers between devices  35.9 us (29%)
  local copies, waits for them, and re-layouts  31.8 us (26%)
  starting transfers between devices  29.5 us (24%)
  other arithmetic  23.4 us (19%)
    unnamed x33, local copies, waits for them, and re-layouts  17.5 us
    ppermute x4, waiting for transfers between devices, extended_2(): lax.ppermute(lax.slice_in_dim(block, 0, width, axis=dim), axis, backward)  15.4 us
    ppermute x4, starting transfers between devices, extended_2(): lax.ppermute(lax.slice_in_dim(block, block.shape[dim] - width, None, axis...  11.7 us
    ppermute x4, waiting for transfers between devices, extended_2(): lax.ppermute(lax.slice_in_dim(block, block.shape[dim] - width, None, axis...  10.3 us
    ppermute x8, waiting for transfers between devices, from_partner(): return lax.ppermute(block, axis, route)  10.2 us
    ppermute x8, starting transfers between devices, from_partner(): return lax.ppermute(block, axis, route)  9.81 us
    ppermute x4, starting transfers between devices, extended_2(): lax.ppermute(lax.slice_in_dim(block, 0, width, axis=dim), axis, backward)  8.02 us
    concatenate x2, local copies, waits for them, and re-layouts, extended_2(): block = jnp.concatenate([low, block, high], axis=dim)  7.9 us
  transfers between devices with their start and end apart: 16, of which 10 were waited for; matrix products, arithmetic and copies ran while one was open for 4% of the time, Pallas kernels for 0%

commit v1 on v0

v1 whole, which is shorter than its diff:
```python
import functools

import jax
import jax.numpy as jnp
from jax import lax
from jax.experimental import pallas as pl
from jax.experimental.pallas import tpu as pltpu
from jax.sharding import PartitionSpec as P

ADVECTION = 0.25
DIFFUSION = 0.2
PRESSURE_GAIN = 0.3
EXPAND_T = 0.4
EXPAND_S = 0.6
CORIOLIS_BASE = 0.1
CORIOLIS_SLOPE = 0.4

LEVELS = 4
UNROLL = 4
FIELDS = 5
ROWS = 32
COLS = 1024
Q_PLANES = FIELDS * LEVELS
M_AT = Q_PLANES
C_AT = Q_PLANES + LEVELS
PLANES = 2 * Q_PLANES + LEVELS
EDGE_PLANES = 4 * Q_PLANES + 3 * LEVELS
SPEED = ADVECTION * 0.25 / DIFFUSION
SLOPE = PRESSURE_GAIN * 0.5 / DIFFUSION

VMEM = pl.BlockSpec(memory_space=pltpu.VMEM)
ANY = pl.BlockSpec(memory_space=pl.ANY)
HBM = pl.BlockSpec(memory_space=pltpu.HBM)


def params(mib, **more):
    return pltpu.CompilerParams(vmem_limit_bytes=mib << 20, **more)


def f32(*shape):
    return jax.ShapeDtypeStruct(shape, jnp.float32)


def iota(dim, shape=(8, 128)):
    return lax.broadcasted_iota(jnp.int32, shape, dim)


def east(x):
    near = pltpu.roll(x, 127, 1)
    return jnp.where(iota(1) == 127, pltpu.roll(near, 7, 0), near)


def west(x):
    near = pltpu.roll(x, 1, 1)
    return jnp.where(iota(1) == 0, pltpu.roll(near, 1, 0), near)


def pressures(fields):
    total, out = None, []
    for k in range(LEVELS):
        density = EXPAND_S * fields[3 * LEVELS + k] - EXPAND_T * fields[2 * LEVELS + k]
        half = 0.5 * density
        out.append(half if total is None else total + half)
        total = density if total is None else total + density
    return out


def coriolis(row, total_rows):
    mirrored = jnp.minimum(row, 2 * total_rows - 1 - row)
    return CORIOLIS_BASE + CORIOLIS_SLOPE * (mirrored.astype(jnp.float32) + 0.5) / total_rows


def update_level(q, qe, qw, qn, qs, p, pe, pw, pn, ps, masks, spin):
    me, mw, mn, ms, m0 = masks
    ae = me * (SPEED * (q[0] + qe[0]))
    aw = mw * (SPEED * (q[0] + qw[0]))
    an = mn * (SPEED * (q[1] + qn[1]))
    a_s = ms * (SPEED * (q[1] + qs[1]))
    centre = m0 - ae + aw - an + a_s
    ke, kw, kn, ks = me - ae, mw + aw, mn - an, ms + a_s
    out = [
        centre * q[f] + ke * qe[f] + kw * qw[f] + kn * qn[f] + ks * qs[f] for f in range(FIELDS)
    ]
    gx = SLOPE * (me * (pe - p) + mw * (p - pw))
    gy = SLOPE * (mn * (pn - p) + ms * (p - ps))
    out[0] = out[0] + (spin * q[1] - gx)
    out[1] = out[1] - (spin * q[0] + gy)
    return out


def face_masks(m, m_e, m_w, m_n, m_s):
    scaled = DIFFUSION * m
    me, mw = scaled * m_e, scaled * m_w
    mn = jnp.zeros_like(m) if m_n is None else scaled * m_n
    ms = jnp.zeros_like(m) if m_s is None else scaled * m_s
    return me, mw, mn, ms, m - ((me + mw) + (mn + ms))


def pick(fields, k):
    return [fields[f * LEVELS + k] for f in range(FIELDS)]


def step_row(q, qn, qs, m, mn, ms, spin, add=None):
    p = pressures(q)
    pn, ps = pressures(qn), pressures(qs)
    out = [None] * Q_PLANES
    for k in range(LEVELS):
        own = pick(q, k)
        masks = face_masks(
            m[k],
            east(m[k]),
            west(m[k]),
            None if mn is None else mn[k],
            None if ms is None else ms[k],
        )
        new = update_level(
            own,
            [east(x) for x in own],
            [west(x) for x in own],
            pick(qn, k),
            pick(qs, k),
            p[k],
            east(p[k]),
            west(p[k]),
            pn[k],
            ps[k],
            masks,
            spin * m[k],
        )
        for f in range(FIELDS):
            i = f * LEVELS + k
            out[i] = new[f] if add is None else new[f] + add[i]
    return out


def row_of(ref, k, tile, r):
    return ref[k, tile, pl.ds(r, 8, stride=8), :]


def rows_kernel(*refs):
    args = refs[:6]
    msg_a, msg_b, scratch, floats, ints, sems = refs[6:]
    low, high, copies = [], [], []
    for side, rows in enumerate((low, high)):
        for f in range(6):
            here = floats.at[side, f] if f < FIELDS else ints.at[side]
            rows.append(here)
            two = pl.ds(6 * side, 2)
            tile = args[f].at[:, 3 * side, :, two, :]
            copies.append(pltpu.make_async_copy(tile, here.at[:, :, two, :], sems.at[side, f]))
    for copy in copies:
        copy.start()
    for copy in copies:
        copy.wait()
    lat = lax.axis_index("lat")
    last = lax.axis_size("lat") - 1
    odd = lax.rem(lat, 2) == 1

    def message(tiles, edge, inner, toward):
        q = [tiles[f][k, :, edge, :] for f in range(FIELDS) for k in range(LEVELS)]
        n = [tiles[f][k, :, inner, :] for f in range(FIELDS) for k in range(LEVELS)]
        m = [tiles[5][k, :, edge, :].astype(jnp.float32) for k in range(LEVELS)]
        mi = [tiles[5][k, :, inner, :].astype(jnp.float32) for k in range(LEVELS)]
        p, pi = pressures(q), pressures(n)
        brought = [None] * Q_PLANES
        for k in range(LEVELS):
            mask = DIFFUSION * (m[k] * mi[k])
            a = mask * (SPEED * (q[LEVELS + k] + n[LEVELS + k])) * toward
            ki, ko = mask + a, a - mask
            for f in range(FIELDS):
                i = f * LEVELS + k
                brought[i] = ki * n[i] + ko * q[i]
            i = LEVELS + k
            brought[i] = brought[i] - toward * (SLOPE * mask * (p[k] - pi[k]))
        return q + m + brought

    top = message(high, 7, 6, 1.0)
    bottom = message(low, 0, 1, -1.0)
    for i in range(PLANES):
        msg_a[pl.ds(8 * i, 8), :] = jnp.where(odd, bottom[i], top[i])
        msg_b[pl.ds(8 * i, 8), :] = jnp.where(odd, top[i], bottom[i])

    @pl.when(lat == last)
    def _():
        lane = iota(1)
        for i in range(PLANES):
            x = jnp.take_along_axis(top[i], 127 - lane, axis=1)
            flip = i < 2 * LEVELS or C_AT <= i < C_AT + 2 * LEVELS
            scratch[pl.ds(8 * i, 8), :] = -x if flip else x
        for s in range(8):
            msg_b[pl.ds(7 - s, PLANES, stride=8), :] = scratch[pl.ds(s, PLANES, stride=8), :]


def inner_kernel(*refs):
    args, outs = refs[:6], refs[6:11]
    edge, cols = refs[11:13]
    floats, ints, ready, first, second, mask, press, faces, sems, out_sems = refs[13:]
    lat = lax.axis_index("lat")
    total = ROWS * lax.axis_size("lat")
    base = lat * ROWS
    lane = iota(1)

    def at(row, per_row, i, off=0):
        start = pl.multiple_of(8 * (row * per_row + i + 1), 8)
        return pl.ds(start + off, 8)

    def beside(ref, row, per_row, i):
        x = ref[at(row, per_row, i), :]
        after = ref[at(row, per_row, i, 1), :]
        before = ref[at(row, per_row, i, -1), :]
        e = pltpu.roll(jnp.where(lane == 0, after, x), 127, 1)
        w = pltpu.roll(jnp.where(lane == 127, before, x), 1, 1)
        return x, e, w

    def fetch(tile):
        return [
            pltpu.make_async_copy(
                args[f].at[:, tile],
                floats.at[tile, f] if f < FIELDS else ints.at[tile],
                sems.at[tile, f],
            )
            for f in range(6)
        ]

    def put(tile):
        return [
            pltpu.make_async_copy(ready.at[tile, f], outs[f].at[:, tile], out_sems.at[tile, f])
            for f in range(FIELDS)
        ]

    def step(source, s, r):
        spin = coriolis(base + r, total)
        levels = []
        for k in range(LEVELS):
            sides = [beside(source, r, Q_PLANES, f * LEVELS + k) for f in range(FIELDS)]
            p, pe, pw = beside(press.at[s], r, LEVELS, k)
            if s == 0:
                m, me, mw = beside(mask, r, LEVELS, k)
                mn, ms = mask[at(r + 1, LEVELS, k), :], mask[at(r - 1, LEVELS, k), :]
                face = face_masks(m, me, mw, mn, ms)
                for i in range(5):
                    faces[r, k, i] = face[i]
            else:
                m = mask[at(r, LEVELS, k), :]
                face = [faces[r, k, i] for i in range(5)]
            new = update_level(
                [x[0] for x in sides],
                [x[1] for x in sides],
                [x[2] for x in sides],
                [source[at(r + 1, Q_PLANES, f * LEVELS + k), :] for f in range(FIELDS)],
                [source[at(r - 1, Q_PLANES, f * LEVELS + k), :] for f in range(FIELDS)],
                p,
                pe,
                pw,
                press[s, at(r + 1, LEVELS, k), :],
                press[s, at(r - 1, LEVELS, k), :],
                face,
                spin * m,
            )
            levels.append(new)
        return [levels[k][f] for f in range(FIELDS) for k in range(LEVELS)]

    def step_one(r, c):
        new = step(first, 0, r)
        for i in range(Q_PLANES):
            second[at(r, Q_PLANES, i), :] = new[i]
        for k, p in enumerate(pressures(new)):
            press[1, at(r, LEVELS, k), :] = p
        return c

    def step_two(r, c):
        new = step(second, 1, r)
        tile = r // 8
        for f in range(FIELDS):
            for k in range(LEVELS):
                ready[tile, f, k, pl.ds(r % 8, 8, stride=8), :] = new[f * LEVELS + k]
        return c

    for tile in range(4):
        for copy in fetch(tile):
            copy.start()

    for tile in range(4):
        for copy in fetch(tile):
            copy.wait()
        for r8 in range(8):
            r = tile * 8 + r8
            q = []
            for f in range(FIELDS):
                for k in range(LEVELS):
                    x = floats[tile, f, k, pl.ds(r8, 8, stride=8), :]
                    first[at(r, Q_PLANES, f * LEVELS + k), :] = x
                    q.append(x)
            p = pressures(q)
            for k in range(LEVELS):
                m = ints[tile, k, pl.ds(r8, 8, stride=8), :].astype(jnp.float32)
                mask[at(r, LEVELS, k), :] = m
                press[0, at(r, LEVELS, k), :] = p[k]
        lax.fori_loop(max(1, 8 * tile - 1), 8 * tile + 7, step_one, 0, unroll=UNROLL)
        lax.fori_loop(max(2, 8 * tile - 2), 8 * tile + 6, step_two, 0, unroll=UNROLL)
        if tile > 0:
            for copy in put(tile - 1):
                copy.start()
    for copy in put(3):
        copy.start()

    big_lane = iota(1, (128, 128))
    for f in range(6):
        tiles = [floats.at[t, f] if f < FIELDS else ints.at[t] for t in range(4)]
        left = [tiles[t][k, pl.ds(0, 8), :] for k in range(LEVELS) for t in range(4)]
        right = [tiles[t][k, pl.ds(56, 8), :] for k in range(LEVELS) for t in range(4)]
        left = jnp.concatenate(left, axis=0).astype(jnp.float32)
        right = jnp.concatenate(right, axis=0).astype(jnp.float32)
        both = jnp.where(big_lane < 4, left, pltpu.roll(right, 8, 1))
        cols[f] = both.T[:8]

    for side in range(2):
        e = 0 if side == 0 else ROWS - 1
        d = 1 if side == 0 else -1
        for i in range(Q_PLANES):
            edge[side, i] = first[at(e, Q_PLANES, i), :]
            edge[side, Q_PLANES + i] = first[at(e + d, Q_PLANES, i), :]
            edge[side, 2 * Q_PLANES + i] = second[at(e + d, Q_PLANES, i), :]
            edge[side, 3 * Q_PLANES + i] = second[at(e + 2 * d, Q_PLANES, i), :]
        for k in range(LEVELS):
            for j in range(3):
                edge[side, 4 * Q_PLANES + j * LEVELS + k] = mask[at(e + j * d, LEVELS, k), :]

    for tile in range(4):
        for copy in put(tile):
            copy.wait()


def columns_kernel(recv_a, recv_b, cols, msg_a, msg_b, halos):
    lat_odd = lax.rem(lax.axis_index("lat"), 2) == 1
    lon_odd = lax.rem(lax.axis_index("lon"), 2) == 1
    lane = iota(1, (PLANES, 128))

    def edges(ref):
        left = ref[pl.ds(0, PLANES, stride=8), :]
        right = ref[pl.ds(7, PLANES, stride=8), :]
        return jnp.where(lane < 4, left, pltpu.roll(right, 8, 1))

    from_a, from_b = edges(recv_a), edges(recv_b)
    south = jnp.where(lat_odd, from_a, from_b)
    north = jnp.where(lat_odd, from_b, from_a)
    gap = jnp.zeros((64 - PLANES, 128), jnp.float32)
    turned = jnp.concatenate([south, gap, north, gap], axis=0).T[:8]
    halo_s = turned
    halo_n = pltpu.roll(turned, 64, 1)
    halos[0] = halo_s
    halos[1] = halo_n
    sub = iota(0)

    def pack(at, corner):
        parts = []
        for group in range(2):
            x = jnp.zeros((8, 128), jnp.float32)
            for j in range(4):
                f = group * 4 + j
                if f < 6:
                    y = pltpu.roll(cols[f], (2 * j - at) % 8, 0)
                    x = jnp.where(sub // 2 == j, y, x)
            parts.append(x)
        parts[1] = jnp.where(sub == 4, pltpu.roll(halo_s, (4 - corner) % 8, 0), parts[1])
        parts[1] = jnp.where(sub == 5, pltpu.roll(halo_n, (5 - corner) % 8, 0), parts[1])
        return parts

    westward, eastward = pack(0, 0), pack(6, 7)
    for g in range(2):
        msg_a[pl.ds(8 * g, 8), :] = jnp.where(lon_odd, westward[g], eastward[g])
        msg_b[pl.ds(8 * g, 8), :] = jnp.where(lon_odd, eastward[g], westward[g])


def border_kernel(*refs):
    recv_a, recv_b, edge = refs[:3]
    tiles, outs = refs[3:8], refs[8:13]
    side = pl.program_id(0)
    lat = lax.axis_index("lat")
    odd = lax.rem(lat, 2) == 1
    total = ROWS * lax.axis_size("lat")
    base = lat * ROWS
    for f in range(FIELDS):
        outs[f][...] = tiles[f][...]

    def run(low):
        e = 0 if low else ROWS - 1
        d = 1 if low else -1
        s = 0 if low else 1
        take_a = odd if low else jnp.logical_not(odd)
        halo = [
            jnp.where(take_a, recv_a[pl.ds(8 * i, 8), :], recv_b[pl.ds(8 * i, 8), :])
            for i in range(PLANES)
        ]
        q_out, m_out, add = halo[:M_AT], halo[M_AT:C_AT], halo[C_AT:]
        q0 = [edge[s, i] for i in range(Q_PLANES)]
        q1 = [edge[s, Q_PLANES + i] for i in range(Q_PLANES)]
        m0, m1, m2 = (
            [edge[s, 4 * Q_PLANES + j * LEVELS + k] for k in range(LEVELS)] for j in range(3)
        )

        def row(q, inward, outward, m, m_in, m_o, at, extra=None):
            spin = coriolis(base + at, total)
            if low:
                return step_row(q, inward, outward, m, m_in, m_o, spin, extra)
            return step_row(q, outward, inward, m, m_o, m_in, spin, extra)

        n_out = row(q_out, q0, q_out, m_out, m0, None, e - d, add)
        n0 = row(q0, q1, q_out, m0, m1, m_out, e)
        n1 = [edge[s, 2 * Q_PLANES + i] for i in range(Q_PLANES)]
        n2 = [edge[s, 3 * Q_PLANES + i] for i in range(Q_PLANES)]
        r0 = row(n0, n1, n_out, m0, m1, m_out, e)
        r1 = row(n1, n2, n0, m1, m2, m0, e + d)
        for f in range(FIELDS):
            for k in range(LEVELS):
                i = f * LEVELS + k
                outs[f][k, 0, pl.ds(e % 8, 8, stride=8), :] = r0[i]
                outs[f][k, 0, pl.ds((e + d) % 8, 8, stride=8), :] = r1[i]

    @pl.when(side == 0)
    def _():
        run(True)

    @pl.when(side == 1)
    def _():
        run(False)


def seam_kernel(*refs):
    recv_a, recv_b, cols, halos = refs[:4]
    outs = refs[9:14]
    left, right, sems = refs[14:]
    loads = []
    for f in range(FIELDS):
        loads.append(pltpu.make_async_copy(outs[f].at[:, :, pl.ds(0, 8), :], left.at[f], sems.at[f]))
        loads.append(
            pltpu.make_async_copy(
                outs[f].at[:, :, pl.ds(56, 8), :], right.at[f], sems.at[FIELDS + f]
            )
        )
    for copy in loads:
        copy.start()

    lon_odd = lax.rem(lax.axis_index("lon"), 2) == 1
    lat = lax.axis_index("lat")
    total = ROWS * lax.axis_size("lat")
    sub, lane = iota(0), iota(1)
    pa = [recv_a[pl.ds(8 * g, 8), :] for g in range(2)]
    pb = [recv_b[pl.ds(8 * g, 8), :] for g in range(2)]
    from_west = [jnp.where(lon_odd, a, b) for a, b in zip(pa, pb)]
    from_east = [jnp.where(lon_odd, b, a) for a, b in zip(pa, pb)]

    h_s, h_n = halos[0], halos[1]
    rim = []
    for g, h in enumerate((h_s, h_n)):
        w = jnp.where(sub == 1, pltpu.roll(from_west[1], (1 - 4 - g) % 8, 0), pltpu.roll(h, 2, 0))
        e = jnp.where(sub == 6, pltpu.roll(from_east[1], (6 - 4 - g) % 8, 0), pltpu.roll(h, 6, 0))
        rim.append((w, e))

    spots = ((0, 0, 0), (33, 1, 0), (64, 0, 1), (97, 1, 1))

    def at_rims(base, plane):
        x = base
        for spot, g, side in spots:
            x = jnp.where(lane == spot, pltpu.roll(rim[g][side], (spot - plane) % 128, 1), x)
        return x

    def spread(f, k):
        group, j = f // 4, f % 4
        own = cols[f]
        w = pltpu.roll(from_west[group], (6 - 2 * j) % 8, 0)
        e = pltpu.roll(from_east[group], (8 - 2 * j) % 8, 0)
        w = pltpu.roll(jnp.where(sub >= 6, w, own), 2, 0)
        e = pltpu.roll(jnp.where(sub < 2, e, own), 6, 0)
        x = jnp.where(
            lane < 64,
            pltpu.roll(w, (1 - 32 * k) % 128, 1),
            pltpu.roll(e, (65 - 32 * k) % 128, 1),
        )
        return at_rims(x, f * LEVELS + k)

    q = [spread(f, k) for f in range(FIELDS) for k in range(LEVELS)]
    row = lax.rem(lane, 64) - 1
    valid = row <= ROWS
    m = [jnp.where(valid, spread(5, k), 0.0) for k in range(LEVELS)]
    zero = jnp.zeros((8, 128), jnp.float32)
    brought = [at_rims(zero, C_AT + i) for i in range(Q_PLANES)]
    spin = coriolis(row + lat * ROWS, total)

    def move(x, d, axis):
        return pltpu.roll(x, d % x.shape[axis], axis)

    def shifted(x):
        return move(x, -1, 0), move(x, 1, 0), move(x, -1, 1), move(x, 1, 1)

    masks = [face_masks(m[k], *shifted(m[k])) for k in range(LEVELS)]
    for s in range(2):
        p = pressures(q)
        new_q = [None] * Q_PLANES
        for k in range(LEVELS):
            own = pick(q, k)
            sides = [shifted(x) for x in own]
            qe, qw, qn, qs = ([x[i] for x in sides] for i in range(4))
            new = update_level(own, qe, qw, qn, qs, p[k], *shifted(p[k]), masks[k], spin * m[k])
            for f in range(FIELDS):
                i = f * LEVELS + k
                new_q[i] = new[f] + brought[i] if s == 0 else new[f]
        q = new_q

    for copy in loads:
        copy.wait()

    big_lane = iota(1, (128, 128))
    gap = jnp.zeros((112, 128), jnp.float32)
    for f in range(FIELDS):
        w, e = zero, zero
        for k in range(LEVELS):
            x = q[f * LEVELS + k]
            here = lane // 32 == k
            w = jnp.where(here, pltpu.roll(x, (32 * k - 1) % 128, 1), w)
            e = jnp.where(here, pltpu.roll(x, (32 * k - 65) % 128, 1), e)
        w, e = pltpu.roll(w, 6, 0), pltpu.roll(e, 2, 0)
        turned = jnp.concatenate([w, gap, e], axis=0).T
        a = left[f].reshape(128, 128)
        b = right[f].reshape(128, 128)
        left[f] = jnp.where(big_lane < 2, turned, a).reshape(LEVELS, 4, 8, 128)
        right[f] = jnp.where(big_lane >= 126, turned, b).reshape(LEVELS, 4, 8, 128)

    stores = []
    for f in range(FIELDS):
        stores.append(pltpu.make_async_copy(left.at[f], outs[f].at[:, :, pl.ds(0, 8), :], sems.at[f]))
        stores.append(
            pltpu.make_async_copy(
                right.at[f], outs[f].at[:, :, pl.ds(56, 8), :], sems.at[FIELDS + f]
            )
        )
    for copy in stores:
        copy.start()
    for copy in stores:
        copy.wait()


def view(x):
    return x.reshape(LEVELS, 4, 8, 8, 128).transpose(0, 1, 3, 2, 4)


def unview(x):
    return x.reshape(LEVELS, 4, 8, 8, 128).transpose(0, 1, 3, 2, 4).reshape(LEVELS, ROWS, COLS)


def routes(lons, lats):
    def at(lon, lat):
        return lon * lats + lat

    def other(i, count, shift):
        return ((i + shift) ^ 1) - shift

    lat_a, lat_b, lon_a, lon_b = [], [], [], []
    for lon in range(lons):
        for lat in range(lats):
            me = at(lon, lat)
            lat_a.append((me, at(lon, lat ^ 1)))
            if lat == lats - 1:
                lat_b.append((me, at(lons - 1 - lon, lat)))
            elif lat > 0:
                lat_b.append((me, at(lon, other(lat, lats, 1))))
            lon_a.append((me, at(lon ^ 1, lat)))
            lon_b.append((me, at(other(lon, lons, 1) % lons, lat)))
    return lat_a, lat_b, lon_a, lon_b


def inner_call(args):
    return pl.pallas_call(
        inner_kernel,
        in_specs=[HBM] * 6,
        out_specs=[HBM] * FIELDS + [VMEM] * 2,
        out_shape=[f32(LEVELS, 4, 64, 128)] * FIELDS
        + [f32(2, EDGE_PLANES, 8, 128), f32(6, 8, 128)],
        scratch_shapes=[
            pltpu.VMEM((4, FIELDS, LEVELS, 64, 128), jnp.float32),
            pltpu.VMEM((4, LEVELS, 64, 128), jnp.int32),
            pltpu.VMEM((4, FIELDS, LEVELS, 64, 128), jnp.float32),
            pltpu.VMEM((8 * (ROWS * Q_PLANES + 2), 128), jnp.float32),
            pltpu.VMEM((8 * (ROWS * Q_PLANES + 2), 128), jnp.float32),
            pltpu.VMEM((8 * (ROWS * LEVELS + 2), 128), jnp.float32),
            pltpu.VMEM((2, 8 * (ROWS * LEVELS + 2), 128), jnp.float32),
            pltpu.VMEM((ROWS, LEVELS, 5, 8, 128), jnp.float32),
            pltpu.SemaphoreType.DMA((4, 6)),
            pltpu.SemaphoreType.DMA((4, FIELDS)),
        ],
        compiler_params=params(62),
        cost_estimate=pl.CostEstimate(flops=26 << 20, bytes_accessed=6 << 20, transcendentals=0),
        name="inner_rows",
    )(*args)


def per_device(*args):
    axes = ("lon", "lat")
    lat_a, lat_b, lon_a, lon_b = routes(lax.axis_size("lon"), lax.axis_size("lat"))
    args = [view(x) for x in args]
    out = f32(LEVELS, 4, 64, 128)
    planes = EDGE_PLANES

    send_a, send_b = pl.pallas_call(
        rows_kernel,
        in_specs=[HBM] * 6,
        out_specs=[VMEM] * 2,
        out_shape=[f32(PLANES * 8, 128)] * 2,
        scratch_shapes=[
            pltpu.VMEM((PLANES * 8, 128), jnp.float32),
            pltpu.VMEM((2, FIELDS, LEVELS, 8, 8, 128), jnp.float32),
            pltpu.VMEM((2, LEVELS, 8, 8, 128), jnp.int32),
            pltpu.SemaphoreType.DMA((2, 6)),
        ],
        compiler_params=params(63),
        cost_estimate=pl.CostEstimate(flops=1 << 20, bytes_accessed=2 << 20, transcendentals=0),
        name="edge_rows",
    )(*args)
    args = [x.reshape(LEVELS, 4, 64, 128) for x in args]
    recv_b = lax.ppermute(send_b, axes, lat_b)
    recv_a = lax.ppermute(send_a, axes, lat_a)

    *inner, edge, cols = inner_call(args)

    send_la, send_lb, halos = pl.pallas_call(
        columns_kernel,
        in_specs=[VMEM] * 3,
        out_specs=[VMEM] * 3,
        out_shape=[f32(16, 128), f32(16, 128), f32(2, 8, 128)],
        compiler_params=params(16),
        name="edge_columns",
    )(recv_a, recv_b, cols)
    recv_lb = lax.ppermute(send_lb, axes, lon_b)
    recv_la = lax.ppermute(send_la, axes, lon_a)

    whole2 = pl.BlockSpec((PLANES * 8, 128), lambda i: (0, 0))
    all_edges = pl.BlockSpec((2, planes, 8, 128), lambda i: (0, 0, 0, 0))
    sides = pl.BlockSpec((LEVELS, 1, 64, 128), lambda i: (0, 3 * i, 0, 0))
    border = pl.pallas_call(
        border_kernel,
        grid=(2,),
        in_specs=[whole2, whole2, all_edges] + [sides] * FIELDS,
        out_specs=[sides] * FIELDS,
        out_shape=[out] * FIELDS,
        input_output_aliases={3 + f: f for f in range(FIELDS)},
        compiler_params=params(24),
        cost_estimate=pl.CostEstimate(flops=4 << 20, bytes_accessed=4 << 20, transcendentals=0),
        name="border_rows",
    )(recv_a, recv_b, edge, *inner)

    final = pl.pallas_call(
        seam_kernel,
        in_specs=[VMEM] * 4 + [ANY] * FIELDS,
        out_specs=[ANY] * FIELDS,
        out_shape=[out] * FIELDS,
        input_output_aliases={4 + f: f for f in range(FIELDS)},
        scratch_shapes=[
            pltpu.VMEM((FIELDS, LEVELS, 4, 8, 128), jnp.float32),
            pltpu.VMEM((FIELDS, LEVELS, 4, 8, 128), jnp.float32),
            pltpu.SemaphoreType.DMA((2 * FIELDS,)),
        ],
        compiler_params=params(16),
        name="seam_columns",
    )(recv_la, recv_lb, cols, halos, *border)
    return tuple(unview(x) for x in final)


def solution(mesh):
    spec = P(None, "lat", "lon")
    return jax.shard_map(
        per_device,
        mesh=mesh,
        in_specs=(spec,) * 6,
        out_specs=(spec,) * 5,
        check_vma=False,
    )
```

time: 124 us -> 31.3 us (0.25); the launches traced: 122 us -> 31 us
  waiting for transfers between devices: 35.9 us -> 0.01 us
  local copies, waits for them, and re-layouts: 31.8 us -> 1.86 us
  other arithmetic: 23.4 us -> 0 us
  starting transfers between devices: 29.5 us -> 11.2 us
  Pallas kernels: 0 us -> 17.2 us
    ppermute x16 -> x4, waiting for transfers between devices: 35.9 us -> 0.01 us  [the longest x1 0.01 us: per_device(): recv_a = lax.ppermute(send_a, axes, lat_a)]
    ppermute x16 -> x4, starting transfers between devices: 29.5 us -> 11.2 us  [the longest x1 6.04 us: per_device(): recv_b = lax.ppermute(send_b, axes, lat_b)]
    pallas_call x0 -> x5, Pallas kernels: none -> 17.2 us  [the longest x1 9 us: inner_call(): pl.pallas_call(inner_kernel, in_specs=[HBM] * 6, out_specs=[HBM] * FIELDS...]
    unnamed x33 -> x6, local copies, waits for them, and re-layouts: 17.5 us -> 1.86 us
    mul x12 -> x0, other arithmetic: 15.3 us -> none  [the longest x2 3.68 us: advance(): face_y * (ADVECTION * speed_y * (0.5 * (north_side + south_side)) - DIFFU...]
    concatenate x2 -> x0, local copies, waits for them, and re-layouts: 7.9 us -> none  [extended_2(): block = jnp.concatenate([low, block, high], axis=dim)]
    slice x7 -> x0, local copies, waits for them, and re-layouts: 4.59 us -> none  [the longest x4 4.08 us: extended_2(): lax.slice_in_dim(block, 0, width, axis=dim)]
    broadcast_in_dim x2 -> x0, other arithmetic: 2.12 us -> none  [advance(): tend_u[None]]
  transfers between devices with their start and end apart: 16 -> 4, of which waited for: 10 -> 0; matrix products, arithmetic and copies ran while one was open for 4% -> 0% of each run, Pallas kernels for 0% -> 38%
where the time goes in v1:
time: 31.3 us; the launch traced here: 31 us
  Pallas kernels  17.2 us (55%)
  starting transfers between devices  11.2 us (36%)
  local copies, waits for them, and re-layouts  1.86 us (6%)
  between operations  0.7 us (2%)
    pallas_call x1, Pallas kernels, inner_call(): pl.pallas_call(inner_kernel, in_specs=[HBM] * 6, out_specs=[HBM] * FIELDS...  9 us
    ppermute x1, starting transfers between devices, per_device(): recv_b = lax.ppermute(send_b, axes, lat_b)  6.04 us
    ppermute x1, starting transfers between devices, per_device(): recv_lb = lax.ppermute(send_lb, axes, lon_b)  4.62 us
    pallas_call x1, Pallas kernels, per_device(): pl.pallas_call(border_kernel, grid=(2,), in_specs=[whole2, whole2, all_ed...  2.9 us
    pallas_call x1, Pallas kernels, per_device(): pl.pallas_call(seam_kernel, in_specs=[VMEM] * 4 + [ANY] * FIELDS, out_spe...  2.55 us
    pallas_call x1, Pallas kernels, per_device(): pl.pallas_call(rows_kernel, in_specs=[HBM] * 6, out_specs=[VMEM] * 2, out...  2.54 us
    unnamed x6, local copies, waits for them, and re-layouts  1.86 us
  transfers between devices with their start and end apart: 4, of which 0 were waited for; matrix products, arithmetic and copies ran while one was open for 0% of the time, Pallas kernels for 38%

profile of v1, /device:TPU:104, one launch (start us, length us, event | category | flops | bytes accessed | tf_op | source)
XLA Modules:
  0.0 31.0 jit_solution(14336997169818111449)
XLA Ops:
  0.6 2.5 %edge_rows.1 = (f32[352,128]{1,0:T(8,128)}, f32[352,128]{1,0:T(8,128)}) custom-call(f32[4,4,8,8,128]{4,3,2,1,0:T(8,128)} %bitcast.60, f32[4,4,8,8,128]{4,3,2,1,0:T(8,128)} %bitcast.62, f32[4,4,8,8,128]{4,3,2,1,0:T(8,128)} %bitcast.64, f32[4,4,8,8,128]{4,3,2,1,0:T(8,128)} %bitcast.66, f32[4,4,8,8,128]{4,3,2,1,0:T(8,128)} %bitcast.68, ...), custom_call_target="tpu_custom_call" | custom-call | flops 1048576 | bytes 2097152 | tf_op jit(solution)/shard_map/edge_rows/pallas_call | solution.py:604
  3.2 0.5 %collective-permute-start = (f32[352,128]{1,0:T(8,128)}, f32[352,128]{1,0:T(8,128)S(1)}, u32[]{:S(2)}, u32[]{:S(2)}) collective-permute-start(f32[352,128]{1,0:T(8,128)} %get-tuple-element.27), channel_id=1, source_target_pairs={{0,1},{1,0},{2,3},{3,2},{4,5},{5,4},{6,7},{7,6},{8,9},{9,8},{10,11... | collective-permute-start | bytes 540680 | tf_op jit(solution)/shard_map/ppermute | solution.py:621
  3.7 6.0 %collective-permute-start.1 = (f32[352,128]{1,0:T(8,128)}, f32[352,128]{1,0:T(8,128)S(1)}, u32[]{:S(2)}, u32[]{:S(2)}) collective-permute-start(f32[352,128]{1,0:T(8,128)} %get-tuple-element.28), channel_id=1, source_target_pairs={{1,2},{2,1},{3,4},{4,3},{5,6},{6,5},{7,8},{8,7},{9,10},{10,9},{11,... | collective-permute-start | bytes 540680 | tf_op jit(solution)/shard_map/ppermute | solution.py:620
  9.8 9.0 %inner_rows.1 = (f32[4,4,64,128]{3,2,1,0:T(8,128)}, f32[4,4,64,128]{3,2,1,0:T(8,128)}, f32[4,4,64,128]{3,2,1,0:T(8,128)}, f32[4,4,64,128]{3,2,1,0:T(8,128)}, f32...) custom-call(f32[4,4,64,128]{3,2,1,0:T(8,128)} %bitcast.61, f32[4,4,64,128]{3,2,1,0:T(8,128)} %bitcast.63, ...), custom_call_target="tpu_custom_call" | custom-call | flops 27262976 | bytes 6291456 | tf_op jit(solution)/shard_map/inner_rows/pallas_call | solution.py:573
  18.8 0.0 collective-permute-done.recv_a.refs_0_
  18.8 0.0 collective-permute-done.1.recv_b.refs_1_
  18.8 0.0 copy-start.1
  18.8 0.7 %copy-done.1 = f32[6,8,128]{2,1,0:T(8,128)S(1)} copy-done((f32[6,8,128]{2,1,0:T(8,128)S(1)}, f32[6,8,128]{2,1,0:T(8,128)}, u32[]{:S(2)}) %copy-start.1) | copy-done | bytes 24600
  19.5 0.2 edge_columns.1
  19.7 0.0 collective-permute-start.2
  19.7 4.6 %collective-permute-start.3 = (f32[16,128]{1,0:T(8,128)S(1)}, f32[16,128]{1,0:T(8,128)S(1)}, u32[]{:S(2)}, u32[]{:S(2)}) collective-permute-start(f32[16,128]{1,0:T(8,128)S(1)} %get-tuple-element.31), channel_id=1, source_target_pairs={{0,240},{1,241},{2,242},{3,243},{4,244},{5,245},{6,246},{7,247},{8... | collective-permute-start | bytes 24584 | tf_op jit(solution)/shard_map/ppermute | solution.py:633
  24.3 0.0 copy-start
  24.3 1.1 %copy-done = f32[2,92,8,128]{3,2,1,0:T(8,128)S(1)} copy-done((f32[2,92,8,128]{3,2,1,0:T(8,128)S(1)}, f32[2,92,8,128]{3,2,1,0:T(8,128)}, u32[]{:S(2)}) %copy-start) | copy-done | bytes 753688
  25.5 0.0 copy-start.2
  25.5 2.9 %border_rows.1 = (f32[4,4,64,128]{3,2,1,0:T(8,128)}, f32[4,4,64,128]{3,2,1,0:T(8,128)}, f32[4,4,64,128]{3,2,1,0:T(8,128)}, f32[4,4,64,128]{3,2,1,0:T(8,128)}, f32[4,4,64,128]{3,2,1,0:T(8,128)}) custom-call(f32[352,128]{1,0:T(8,128)S(1)} %collective-permute-done.recv_a.refs_0_, ...), custom_call_target="tpu_custom_call", output_to_operand_aliasing={{0}: (3, {}), {1}: (4, {}), {2}: (5, {}), {3}: (6, {}), {4}... | custom-call | flops 4194304 | bytes 4194304 | tf_op jit(solution)/shard_map/border_rows/pallas_call | solution.py:639
  28.4 0.0 collective-permute-done.2.refs_0_
  28.4 0.0 collective-permute-done.3.refs_1_
  28.4 0.0 copy-done.2
  28.4 2.6 %seam_columns.1 = (f32[4,4,64,128]{3,2,1,0:T(8,128)}, f32[4,4,64,128]{3,2,1,0:T(8,128)}, f32[4,4,64,128]{3,2,1,0:T(8,128)}, f32[4,4,64,128]{3,2,1,0:T(8,128)}, f32[4,4,64,128]{3,2,1,0:T(8,128)}) custom-call(f32[16,128]{1,0:T(8,128)S(1)} %collective-permute-done.2.refs_0_, ...), custom_call_target="tpu_custom_call", output_to_operand_aliasing={{0}: (4, {}), {1}: (5, {}), {2}: (6, {}), {3}: (7, {}), {4}... | custom-call | tf_op jit(solution)/shard_map/seam_columns/pallas_call | solution.py:651
Async XLA Ops:
  3.2 15.6 %collective-permute-start = (f32[352,128]{1,0:T(8,128)}, f32[352,128]{1,0:T(8,128)S(1)}, u32[]{:S(2)}, u32[]{:S(2)}) collective-permute-start(f32[352,128]{1,0:T(8,128)} %get-tuple-element.27), channel_id=1, source_target_pairs={{0,1},{1,0},{2,3},{3,2},{4,5},{5,4},{6,7},{7,6},{8,9},{9,8},{10,11... | collective-permute-start | bytes 540680 | tf_op jit(solution)/shard_map/ppermute | solution.py:621
  3.7 15.1 %collective-permute-start.1 = (f32[352,128]{1,0:T(8,128)}, f32[352,128]{1,0:T(8,128)S(1)}, u32[]{:S(2)}, u32[]{:S(2)}) collective-permute-start(f32[352,128]{1,0:T(8,128)} %get-tuple-element.28), channel_id=1, source_target_pairs={{1,2},{2,1},{3,4},{4,3},{5,6},{6,5},{7,8},{8,7},{9,10},{10,9},{11,... | collective-permute-start | bytes 540680 | tf_op jit(solution)/shard_map/ppermute | solution.py:620
  18.8 0.7 %copy-start.1 = (f32[6,8,128]{2,1,0:T(8,128)S(1)}, f32[6,8,128]{2,1,0:T(8,128)}, u32[]{:S(2)}) copy-start(f32[6,8,128]{2,1,0:T(8,128)} %get-tuple-element.29.cols.refs_2_) | copy-start | bytes 73732
  19.7 8.7 %collective-permute-start.2 = (f32[16,128]{1,0:T(8,128)S(1)}, f32[16,128]{1,0:T(8,128)S(1)}, u32[]{:S(2)}, u32[]{:S(2)}) collective-permute-start(f32[16,128]{1,0:T(8,128)S(1)} %get-tuple-element.30), channel_id=1, source_target_pairs={{0,16},{1,17},{2,18},{3,19},{4,20},{5,21},{6,22},{7,23},{8,24},{9,... | collective-permute-start | bytes 24584 | tf_op jit(solution)/shard_map/ppermute | solution.py:634
  19.7 8.7 %collective-permute-start.3 = (f32[16,128]{1,0:T(8,128)S(1)}, f32[16,128]{1,0:T(8,128)S(1)}, u32[]{:S(2)}, u32[]{:S(2)}) collective-permute-start(f32[16,128]{1,0:T(8,128)S(1)} %get-tuple-element.31), channel_id=1, source_target_pairs={{0,240},{1,241},{2,242},{3,243},{4,244},{5,245},{6,246},{7,247},{8... | collective-permute-start | bytes 24584 | tf_op jit(solution)/shard_map/ppermute | solution.py:633
  24.3 1.1 %copy-start = (f32[2,92,8,128]{3,2,1,0:T(8,128)S(1)}, f32[2,92,8,128]{3,2,1,0:T(8,128)}, u32[]{:S(2)}) copy-start(f32[2,92,8,128]{3,2,1,0:T(8,128)} %get-tuple-element.33.refs_2_) | copy-start | bytes 2260996
  25.5 2.9 %copy-start.2 = (f32[6,8,128]{2,1,0:T(8,128)S(1)}, f32[6,8,128]{2,1,0:T(8,128)}, u32[]{:S(2)}) copy-start(f32[6,8,128]{2,1,0:T(8,128)} %get-tuple-element.29.cols.refs_2_) | copy-start | bytes 73732

commit v2 on v1

--- a/solution.py
+++ b/solution.py
@@ -16,7 +16,8 @@
 CORIOLIS_SLOPE = 0.4
 
 LEVELS = 4
-UNROLL = 4
+UNROLL = 8
+LIMIT = 50.3
 FIELDS = 5
 ROWS = 32
 COLS = 1024
@@ -29,12 +30,11 @@
 SLOPE = PRESSURE_GAIN * 0.5 / DIFFUSION
 
 VMEM = pl.BlockSpec(memory_space=pltpu.VMEM)
-ANY = pl.BlockSpec(memory_space=pl.ANY)
 HBM = pl.BlockSpec(memory_space=pltpu.HBM)
 
 
 def params(mib, **more):
-    return pltpu.CompilerParams(vmem_limit_bytes=mib << 20, **more)
+    return pltpu.CompilerParams(vmem_limit_bytes=int(mib * (1 << 20)), **more)
 
 
 def f32(*shape):
@@ -139,19 +139,23 @@
 
 def rows_kernel(*refs):
     args = refs[:6]
-    msg_a, msg_b, scratch, floats, ints, sems = refs[6:]
-    low, high, copies = [], [], []
-    for side, rows in enumerate((low, high)):
-        for f in range(6):
-            here = floats.at[side, f] if f < FIELDS else ints.at[side]
-            rows.append(here)
-            two = pl.ds(6 * side, 2)
-            tile = args[f].at[:, 3 * side, :, two, :]
-            copies.append(pltpu.make_async_copy(tile, here.at[:, :, two, :], sems.at[side, f]))
-    for copy in copies:
-        copy.start()
-    for copy in copies:
-        copy.wait()
+    msg_a, msg_b = refs[6:8]
+    kept = refs[8:14]
+    scratch, sems = refs[14:]
+    copies = [
+        [
+            pltpu.make_async_copy(args[f].at[:, t], kept[f].at[:, t], sems.at[t, f])
+            for f in range(6)
+        ]
+        for t in range(4)
+    ]
+    for t in (0, 3, 1, 2):
+        for copy in copies[t]:
+            copy.start()
+    for t in (0, 3):
+        for copy in copies[t]:
+            copy.wait()
+    low, high = ([x.at[:, t] for x in kept] for t in (0, 3))
     lat = lax.axis_index("lat")
     last = lax.axis_size("lat") - 1
     odd = lax.rem(lat, 2) == 1
@@ -190,11 +194,15 @@
         for s in range(8):
             msg_b[pl.ds(7 - s, PLANES, stride=8), :] = scratch[pl.ds(s, PLANES, stride=8), :]
 
+    for t in (1, 2):
+        for copy in copies[t]:
+            copy.wait()
+
 
 def inner_kernel(*refs):
     args, outs = refs[:6], refs[6:11]
     edge, cols = refs[11:13]
-    floats, ints, ready, first, second, mask, press, faces, sems, out_sems = refs[13:]
+    ready, first, second, mask, press, faces, out_sems = refs[13:]
     lat = lax.axis_index("lat")
     total = ROWS * lax.axis_size("lat")
     base = lat * ROWS
@@ -211,16 +219,6 @@
         e = pltpu.roll(jnp.where(lane == 0, after, x), 127, 1)
         w = pltpu.roll(jnp.where(lane == 127, before, x), 1, 1)
         return x, e, w
-
-    def fetch(tile):
-        return [
-            pltpu.make_async_copy(
-                args[f].at[:, tile],
-                floats.at[tile, f] if f < FIELDS else ints.at[tile],
-                sems.at[tile, f],
-            )
-            for f in range(6)
-        ]
 
     def put(tile):
         return [
@@ -277,23 +275,17 @@
         return c
 
     for tile in range(4):
-        for copy in fetch(tile):
-            copy.start()
-
-    for tile in range(4):
-        for copy in fetch(tile):
-            copy.wait()
         for r8 in range(8):
             r = tile * 8 + r8
             q = []
             for f in range(FIELDS):
                 for k in range(LEVELS):
-                    x = floats[tile, f, k, pl.ds(r8, 8, stride=8), :]
+                    x = row_of(args[f], k, tile, r8)
                     first[at(r, Q_PLANES, f * LEVELS + k), :] = x
                     q.append(x)
             p = pressures(q)
             for k in range(LEVELS):
-                m = ints[tile, k, pl.ds(r8, 8, stride=8), :].astype(jnp.float32)
+                m = row_of(args[5], k, tile, r8).astype(jnp.float32)
                 mask[at(r, LEVELS, k), :] = m
                 press[0, at(r, LEVELS, k), :] = p[k]
         lax.fori_loop(max(1, 8 * tile - 1), 8 * tile + 7, step_one, 0, unroll=UNROLL)
@@ -306,11 +298,8 @@
 
     big_lane = iota(1, (128, 128))
     for f in range(6):
-        tiles = [floats.at[t, f] if f < FIELDS else ints.at[t] for t in range(4)]
-        left = [tiles[t][k, pl.ds(0, 8), :] for k in range(LEVELS) for t in range(4)]
-        right = [tiles[t][k, pl.ds(56, 8), :] for k in range(LEVELS) for t in range(4)]
-        left = jnp.concatenate(left, axis=0).astype(jnp.float32)
-        right = jnp.concatenate(right, axis=0).astype(jnp.float32)
+        left = args[f][:, :, pl.ds(0, 8), :].reshape(128, 128).astype(jnp.float32)
+        right = args[f][:, :, pl.ds(56, 8), :].reshape(128, 128).astype(jnp.float32)
         both = jnp.where(big_lane < 4, left, pltpu.roll(right, 8, 1))
         cols[f] = both.T[:8]
 
@@ -373,33 +362,36 @@
 
 
 def border_kernel(*refs):
-    recv_a, recv_b, edge = refs[:3]
-    tiles, outs = refs[3:8], refs[8:13]
-    side = pl.program_id(0)
+    recv_a, recv_b, edge_hbm = refs[:3]
+    outs = refs[8:13]
+    edge, rows, sems, out_sems = refs[13:]
+    loads = [pltpu.make_async_copy(edge_hbm.at[s], edge.at[s], sems.at[s]) for s in range(2)]
+    for copy in loads:
+        copy.start()
     lat = lax.axis_index("lat")
     odd = lax.rem(lat, 2) == 1
     total = ROWS * lax.axis_size("lat")
     base = lat * ROWS
-    for f in range(FIELDS):
-        outs[f][...] = tiles[f][...]
-
-    def run(low):
+    stores = []
+    for s in range(2):
+        low = s == 0
         e = 0 if low else ROWS - 1
         d = 1 if low else -1
-        s = 0 if low else 1
         take_a = odd if low else jnp.logical_not(odd)
         halo = [
             jnp.where(take_a, recv_a[pl.ds(8 * i, 8), :], recv_b[pl.ds(8 * i, 8), :])
             for i in range(PLANES)
         ]
         q_out, m_out, add = halo[:M_AT], halo[M_AT:C_AT], halo[C_AT:]
-        q0 = [edge[s, i] for i in range(Q_PLANES)]
-        q1 = [edge[s, Q_PLANES + i] for i in range(Q_PLANES)]
+        loads[s].wait()
+        q0, q1, n1, n2 = (
+            [edge[s, j * Q_PLANES + i] for i in range(Q_PLANES)] for j in range(4)
+        )
         m0, m1, m2 = (
             [edge[s, 4 * Q_PLANES + j * LEVELS + k] for k in range(LEVELS)] for j in range(3)
         )
 
-        def row(q, inward, outward, m, m_in, m_o, at, extra=None):
+        def row(q, inward, outward, m, m_in, m_o, at, extra=None, low=low):
             spin = coriolis(base + at, total)
             if low:
                 return step_row(q, inward, outward, m, m_in, m_o, spin, extra)
@@ -407,29 +399,72 @@
 
         n_out = row(q_out, q0, q_out, m_out, m0, None, e - d, add)
         n0 = row(q0, q1, q_out, m0, m1, m_out, e)
-        n1 = [edge[s, 2 * Q_PLANES + i] for i in range(Q_PLANES)]
-        n2 = [edge[s, 3 * Q_PLANES + i] for i in range(Q_PLANES)]
         r0 = row(n0, n1, n_out, m0, m1, m_out, e)
         r1 = row(n1, n2, n0, m1, m2, m0, e + d)
+        two = pl.ds(6 * s, 2)
         for f in range(FIELDS):
             for k in range(LEVELS):
                 i = f * LEVELS + k
-                outs[f][k, 0, pl.ds(e % 8, 8, stride=8), :] = r0[i]
-                outs[f][k, 0, pl.ds((e + d) % 8, 8, stride=8), :] = r1[i]
-
-    @pl.when(side == 0)
-    def _():
-        run(True)
-
-    @pl.when(side == 1)
-    def _():
-        run(False)
+                rows[s, f, k, :, e % 8, :] = r0[i]
+                rows[s, f, k, :, (e + d) % 8, :] = r1[i]
+            stores.append(
+                pltpu.make_async_copy(
+                    rows.at[s, f, :, :, two, :],
+                    outs[f].at[:, 3 * s, :, two, :],
+                    out_sems.at[s, f],
+                )
+            )
+            stores[-1].start()
+    for copy in stores:
+        copy.wait()
+
+
+SPOTS = (0, 33, 64, 97)
+
+
+def spots(west_s, west_n, east_s, east_n):
+    lane = iota(1)
+    out = jnp.zeros((8, 128), jnp.float32)
+    for spot, x in zip(SPOTS, (west_s, west_n, east_s, east_n)):
+        here = jnp.logical_and(lane >= spot, lane < spot + C_AT)
+        out = jnp.where(here, pltpu.roll(x, spot, 1) if spot else x, out)
+    return out
+
+
+def at_spot(lane):
+    hit = lane == SPOTS[0]
+    for spot in SPOTS[1:]:
+        hit = jnp.logical_or(hit, lane == spot)
+    return hit
+
+
+def seam_own_kernel(cols, halos, own):
+    lane = iota(1)
+    h_s, h_n = halos[0], halos[1]
+    w_s, w_n = pltpu.roll(h_s, 2, 0), pltpu.roll(h_n, 2, 0)
+    e_s, e_n = pltpu.roll(h_s, 6, 0), pltpu.roll(h_n, 6, 0)
+    here = at_spot(lane)
+    rim = spots(w_s, w_n, e_s, e_n)
+    for f in range(6):
+        w, e = pltpu.roll(cols[f], 2, 0), pltpu.roll(cols[f], 6, 0)
+        for k in range(LEVELS):
+            i = f * LEVELS + k
+            x = jnp.where(
+                lane < 64,
+                pltpu.roll(w, (1 - 32 * k) % 128, 1),
+                pltpu.roll(e, (65 - 32 * k) % 128, 1),
+            )
+            own[i] = jnp.where(here, pltpu.roll(rim, (128 - i) % 128, 1), x)
+    back = 128 - C_AT
+    rim = spots(*(pltpu.roll(x, back, 1) for x in (w_s, w_n, e_s, e_n)))
+    for i in range(Q_PLANES):
+        own[C_AT + i] = jnp.where(here, pltpu.roll(rim, (128 - i) % 128, 1), 0.0)
 
 
 def seam_kernel(*refs):
-    recv_a, recv_b, cols, halos = refs[:4]
-    outs = refs[9:14]
-    left, right, sems = refs[14:]
+    recv_a, recv_b, own = refs[:3]
+    outs = refs[8:13]
+    left, right, sems = refs[13:]
     loads = []
     for f in range(FIELDS):
         loads.append(pltpu.make_async_copy(outs[f].at[:, :, pl.ds(0, 8), :], left.at[f], sems.at[f]))
@@ -448,43 +483,32 @@
     pa = [recv_a[pl.ds(8 * g, 8), :] for g in range(2)]
     pb = [recv_b[pl.ds(8 * g, 8), :] for g in range(2)]
     from_west = [jnp.where(lon_odd, a, b) for a, b in zip(pa, pb)]
-    from_east = [jnp.where(lon_odd, b, a) for a, b in zip(pa, pb)]
-
-    h_s, h_n = halos[0], halos[1]
-    rim = []
-    for g, h in enumerate((h_s, h_n)):
-        w = jnp.where(sub == 1, pltpu.roll(from_west[1], (1 - 4 - g) % 8, 0), pltpu.roll(h, 2, 0))
-        e = jnp.where(sub == 6, pltpu.roll(from_east[1], (6 - 4 - g) % 8, 0), pltpu.roll(h, 6, 0))
-        rim.append((w, e))
-
-    spots = ((0, 0, 0), (33, 1, 0), (64, 0, 1), (97, 1, 1))
-
-    def at_rims(base, plane):
-        x = base
-        for spot, g, side in spots:
-            x = jnp.where(lane == spot, pltpu.roll(rim[g][side], (spot - plane) % 128, 1), x)
-        return x
-
-    def spread(f, k):
+    from_east = [pltpu.roll(jnp.where(lon_odd, b, a), 64, 1) for a, b in zip(pa, pb)]
+
+    w_s, w_n = pltpu.roll(from_west[1], 5, 0), pltpu.roll(from_west[1], 4, 0)
+    turned = pltpu.roll(from_east[1], 64, 1)
+    e_s, e_n = pltpu.roll(turned, 2, 0), pltpu.roll(turned, 1, 0)
+    corner = spots(w_s, w_n, e_s, e_n)
+    at_corner = jnp.logical_and(at_spot(lane), sub == jnp.where(lane < 64, 1, 6))
+    row = lax.rem(lane, 64) - 1
+    inside = jnp.logical_and(row >= 0, row < ROWS)
+    outer = jnp.logical_and(inside, sub // 2 == jnp.where(lane < 64, 0, 3))
+
+    q, m = [], []
+    for f in range(6):
         group, j = f // 4, f % 4
-        own = cols[f]
-        w = pltpu.roll(from_west[group], (6 - 2 * j) % 8, 0)
-        e = pltpu.roll(from_east[group], (8 - 2 * j) % 8, 0)
-        w = pltpu.roll(jnp.where(sub >= 6, w, own), 2, 0)
-        e = pltpu.roll(jnp.where(sub < 2, e, own), 6, 0)
-        x = jnp.where(
-            lane < 64,
-            pltpu.roll(w, (1 - 32 * k) % 128, 1),
-            pltpu.roll(e, (65 - 32 * k) % 128, 1),
-        )
-        return at_rims(x, f * LEVELS + k)
-
-    q = [spread(f, k) for f in range(FIELDS) for k in range(LEVELS)]
-    row = lax.rem(lane, 64) - 1
-    valid = row <= ROWS
-    m = [jnp.where(valid, spread(5, k), 0.0) for k in range(LEVELS)]
-    zero = jnp.zeros((8, 128), jnp.float32)
-    brought = [at_rims(zero, C_AT + i) for i in range(Q_PLANES)]
+        w = pltpu.roll(from_west[group], (8 - 2 * j) % 8, 0)
+        e = pltpu.roll(from_east[group], (6 - 2 * j) % 8, 0)
+        both = jnp.where(sub < 2, w, e)
+        for k in range(LEVELS):
+            i = f * LEVELS + k
+            x = jnp.where(outer, pltpu.roll(both, (1 - 32 * k) % 128, 1), own[i])
+            x = jnp.where(at_corner, pltpu.roll(corner, (128 - i) % 128, 1), x)
+            if f < FIELDS:
+                q.append(x)
+            else:
+                m.append(jnp.where(row <= ROWS, x, 0.0))
+    brought = [own[C_AT + i] for i in range(Q_PLANES)]
     spin = coriolis(row + lat * ROWS, total)
 
     def move(x, d, axis):
@@ -498,10 +522,10 @@
         p = pressures(q)
         new_q = [None] * Q_PLANES
         for k in range(LEVELS):
-            own = pick(q, k)
-            sides = [shifted(x) for x in own]
+            mine = pick(q, k)
+            sides = [shifted(x) for x in mine]
             qe, qw, qn, qs = ([x[i] for x in sides] for i in range(4))
-            new = update_level(own, qe, qw, qn, qs, p[k], *shifted(p[k]), masks[k], spin * m[k])
+            new = update_level(mine, qe, qw, qn, qs, p[k], *shifted(p[k]), masks[k], spin * m[k])
             for f in range(FIELDS):
                 i = f * LEVELS + k
                 new_q[i] = new[f] + brought[i] if s == 0 else new[f]
@@ -509,11 +533,10 @@
 
     for copy in loads:
         copy.wait()
-
     big_lane = iota(1, (128, 128))
     gap = jnp.zeros((112, 128), jnp.float32)
     for f in range(FIELDS):
-        w, e = zero, zero
+        w = e = jnp.zeros((8, 128), jnp.float32)
         for k in range(LEVELS):
             x = q[f * LEVELS + k]
             here = lane // 32 == k
@@ -525,7 +548,6 @@
         b = right[f].reshape(128, 128)
         left[f] = jnp.where(big_lane < 2, turned, a).reshape(LEVELS, 4, 8, 128)
         right[f] = jnp.where(big_lane >= 126, turned, b).reshape(LEVELS, 4, 8, 128)
-
     stores = []
     for f in range(FIELDS):
         stores.append(pltpu.make_async_copy(left.at[f], outs[f].at[:, :, pl.ds(0, 8), :], sems.at[f]))
@@ -572,23 +594,20 @@
 def inner_call(args):
     return pl.pallas_call(
         inner_kernel,
-        in_specs=[HBM] * 6,
+        in_specs=[VMEM] * 6,
         out_specs=[HBM] * FIELDS + [VMEM] * 2,
         out_shape=[f32(LEVELS, 4, 64, 128)] * FIELDS
         + [f32(2, EDGE_PLANES, 8, 128), f32(6, 8, 128)],
         scratch_shapes=[
-            pltpu.VMEM((4, FIELDS, LEVELS, 64, 128), jnp.float32),
-            pltpu.VMEM((4, LEVELS, 64, 128), jnp.int32),
             pltpu.VMEM((4, FIELDS, LEVELS, 64, 128), jnp.float32),
             pltpu.VMEM((8 * (ROWS * Q_PLANES + 2), 128), jnp.float32),
             pltpu.VMEM((8 * (ROWS * Q_PLANES + 2), 128), jnp.float32),
             pltpu.VMEM((8 * (ROWS * LEVELS + 2), 128), jnp.float32),
             pltpu.VMEM((2, 8 * (ROWS * LEVELS + 2), 128), jnp.float32),
             pltpu.VMEM((ROWS, LEVELS, 5, 8, 128), jnp.float32),
-            pltpu.SemaphoreType.DMA((4, 6)),
             pltpu.SemaphoreType.DMA((4, FIELDS)),
         ],
-        compiler_params=params(62),
+        compiler_params=params(32),
         cost_estimate=pl.CostEstimate(flops=26 << 20, bytes_accessed=6 << 20, transcendentals=0),
         name="inner_rows",
     )(*args)
@@ -601,18 +620,18 @@
     out = f32(LEVELS, 4, 64, 128)
     planes = EDGE_PLANES
 
-    send_a, send_b = pl.pallas_call(
+    split = (LEVELS, 4, 8, 8, 128)
+    kept = [jax.ShapeDtypeStruct(split, x.dtype) for x in args]
+    send_a, send_b, *args = pl.pallas_call(
         rows_kernel,
         in_specs=[HBM] * 6,
-        out_specs=[VMEM] * 2,
-        out_shape=[f32(PLANES * 8, 128)] * 2,
+        out_specs=[VMEM] * 8,
+        out_shape=[f32(PLANES * 8, 128)] * 2 + kept,
         scratch_shapes=[
             pltpu.VMEM((PLANES * 8, 128), jnp.float32),
-            pltpu.VMEM((2, FIELDS, LEVELS, 8, 8, 128), jnp.float32),
-            pltpu.VMEM((2, LEVELS, 8, 8, 128), jnp.int32),
-            pltpu.SemaphoreType.DMA((2, 6)),
+            pltpu.SemaphoreType.DMA((4, 6)),
         ],
-        compiler_params=params(63),
+        compiler_params=params(LIMIT),
         cost_estimate=pl.CostEstimate(flops=1 << 20, bytes_accessed=2 << 20, transcendentals=0),
         name="edge_rows",
     )(*args)
@@ -633,27 +652,39 @@
     recv_lb = lax.ppermute(send_lb, axes, lon_b)
     recv_la = lax.ppermute(send_la, axes, lon_a)
 
-    whole2 = pl.BlockSpec((PLANES * 8, 128), lambda i: (0, 0))
-    all_edges = pl.BlockSpec((2, planes, 8, 128), lambda i: (0, 0, 0, 0))
-    sides = pl.BlockSpec((LEVELS, 1, 64, 128), lambda i: (0, 3 * i, 0, 0))
     border = pl.pallas_call(
         border_kernel,
-        grid=(2,),
-        in_specs=[whole2, whole2, all_edges] + [sides] * FIELDS,
-        out_specs=[sides] * FIELDS,
-        out_shape=[out] * FIELDS,
+        in_specs=[VMEM] * 2 + [HBM] * (1 + FIELDS),
+        out_specs=[HBM] * FIELDS,
+        out_shape=[f32(*split)] * FIELDS,
         input_output_aliases={3 + f: f for f in range(FIELDS)},
+        scratch_shapes=[
+            pltpu.VMEM((2, planes, 8, 128), jnp.float32),
+            pltpu.VMEM((2, FIELDS, LEVELS, 8, 8, 128), jnp.float32),
+            pltpu.SemaphoreType.DMA((2,)),
+            pltpu.SemaphoreType.DMA((2, FIELDS)),
+        ],
         compiler_params=params(24),
         cost_estimate=pl.CostEstimate(flops=4 << 20, bytes_accessed=4 << 20, transcendentals=0),
         name="border_rows",
-    )(recv_a, recv_b, edge, *inner)
+    )(recv_a, recv_b, edge, *(x.reshape(LEVELS, 4, 8, 8, 128) for x in inner))
+
+    own = pl.pallas_call(
+        seam_own_kernel,
+        in_specs=[VMEM] * 2,
+        out_specs=VMEM,
+        out_shape=f32(PLANES, 8, 128),
+        compiler_params=params(16),
+        cost_estimate=pl.CostEstimate(flops=1 << 20, bytes_accessed=1 << 18, transcendentals=0),
+        name="seam_own",
+    )(cols, halos)
 
     final = pl.pallas_call(
         seam_kernel,
-        in_specs=[VMEM] * 4 + [ANY] * FIELDS,
-        out_specs=[ANY] * FIELDS,
+        in_specs=[VMEM] * 3 + [HBM] * FIELDS,
+        out_specs=[HBM] * FIELDS,
         out_shape=[out] * FIELDS,
-        input_output_aliases={4 + f: f for f in range(FIELDS)},
+        input_output_aliases={3 + f: f for f in range(FIELDS)},
         scratch_shapes=[
             pltpu.VMEM((FIELDS, LEVELS, 4, 8, 128), jnp.float32),
             pltpu.VMEM((FIELDS, LEVELS, 4, 8, 128), jnp.float32),
@@ -661,7 +692,7 @@
         ],
         compiler_params=params(16),
         name="seam_columns",
-    )(recv_la, recv_lb, cols, halos, *border)
+    )(recv_la, recv_lb, own, *(x.reshape(LEVELS, 4, 64, 128) for x in border))
     return tuple(unview(x) for x in final)
 
 

time: 31.3 us -> 28.2 us (0.901)
  the two profiles are of different devices: /device:TPU:104 before, /device:TPU:232 now
where the time goes in v2:
time: 28.2 us; the launch traced here: 28.1 us
  Pallas kernels  14.2 us (50%)
  starting transfers between devices  9.76 us (35%)
  waiting for transfers between devices  3.4 us (12%)
  between operations  0.69 us (2%)
    pallas_call x1, Pallas kernels, inner_call(): pl.pallas_call(inner_kernel, in_specs=[VMEM] * 6, out_specs=[HBM] * FIELD...  6.38 us
    ppermute x1, starting transfers between devices, per_device(): recv_b = lax.ppermute(send_b, axes, lat_b)  5.84 us
    ppermute x1, starting transfers between devices, per_device(): recv_lb = lax.ppermute(send_lb, axes, lon_b)  3.56 us
    pallas_call x1, Pallas kernels, per_device(): pl.pallas_call(seam_kernel, in_specs=[VMEM] * 3 + [HBM] * FIELDS, out_spe...  2.74 us
    pallas_call x1, Pallas kernels, per_device(): pl.pallas_call(rows_kernel, in_specs=[HBM] * 6, out_specs=[VMEM] * 8, out...  2.67 us
    ppermute x1, waiting for transfers between devices, per_device(): recv_b = lax.ppermute(send_b, axes, lat_b)  2.43 us
    pallas_call x1, Pallas kernels, per_device(): pl.pallas_call(border_kernel, in_specs=[VMEM] * 2 + [HBM] * (1 + FIELDS),...  2 us
    ppermute x1, waiting for transfers between devices, per_device(): recv_lb = lax.ppermute(send_lb, axes, lon_b)  0.97 us
  transfers between devices with their start and end apart: 4, of which 2 were waited for; matrix products, arithmetic and copies ran while one was open for 0% of the time, Pallas kernels for 31%

profile of v2, /device:TPU:232, one launch (start us, length us, event | category | flops | bytes accessed | tf_op | source)
XLA Modules:
  0.0 28.1 jit_solution(16794117860812016330)
XLA Ops:
  0.6 2.7 %edge_rows.1 = (f32[352,128]{1,0:T(8,128)S(1)}, f32[352,128]{1,0:T(8,128)S(1)}, f32[4,4,8,8,128]{4,3,2,1,0:T(8,128)S(1)}, f32[4,4,8,8,128]{4,3,2,1,0:T(8,128)S(1...) custom-call(f32[4,4,8,8,128]{4,3,2,1,0:T(8,128)} %bitcast.80, ...), custom_call_target="tpu_custom_call" | custom-call | flops 1048576 | bytes 2097152 | tf_op jit(solution)/shard_map/edge_rows/pallas_call | solution.py:625
  3.3 0.4 %collective-permute-start = (f32[352,128]{1,0:T(8,128)S(1)}, f32[352,128]{1,0:T(8,128)S(1)}, u32[]{:S(2)}, u32[]{:S(2)}) collective-permute-start(f32[352,128]{1,0:T(8,128)S(1)} %get-tuple-element.33), channel_id=1, source_target_pairs={{0,1},{1,0},{2,3},{3,2},{4,5},{5,4},{6,7},{7,6},{8,9},{9,8},{10,11... | collective-permute-start | bytes 540680 | tf_op jit(solution)/shard_map/ppermute | solution.py:640
  3.7 5.8 %collective-permute-start.1 = (f32[352,128]{1,0:T(8,128)S(1)}, f32[352,128]{1,0:T(8,128)S(1)}, u32[]{:S(2)}, u32[]{:S(2)}) collective-permute-start(f32[352,128]{1,0:T(8,128)S(1)} %get-tuple-element.34), channel_id=1, source_target_pairs={{1,2},{2,1},{3,4},{4,3},{5,6},{6,5},{7,8},{8,7},{9,10},{10,9},{11,... | collective-permute-start | bytes 540680 | tf_op jit(solution)/shard_map/ppermute | solution.py:639
  9.5 6.4 %inner_rows.1 = (f32[4,4,64,128]{3,2,1,0:T(8,128)}, f32[4,4,64,128]{3,2,1,0:T(8,128)}, f32[4,4,64,128]{3,2,1,0:T(8,128)}, f32[4,4,64,128]{3,2,1,0:T(8,128)}, f32...) custom-call(f32[4,4,64,128]{3,2,1,0:T(8,128)S(1)} %bitcast.59, ...), custom_call_target="tpu_custom_call" | custom-call | flops 27262976 | bytes 6291456 | tf_op jit(solution)/shard_map/inner_rows/pallas_call | solution.py:595
  15.9 0.0 collective-permute-done.recv_a.refs_0_
  15.9 2.4 %collective-permute-done.1.recv_b.refs_1_ = f32[352,128]{1,0:T(8,128)S(1)} collective-permute-done((f32[352,128]{1,0:T(8,128)S(1)}, f32[352,128]{1,0:T(8,128)S(1)}, u32[]{:S(2)}, u32[]{:S(2)}) %collective-permute-start.1) | collective-permute-done | bytes 180256 | tf_op jit(solution)/shard_map/ppermute | solution.py:639
  18.4 0.2 edge_columns.1
  18.6 0.0 collective-permute-start.2
  18.6 3.6 %collective-permute-start.3 = (f32[16,128]{1,0:T(8,128)S(1)}, f32[16,128]{1,0:T(8,128)S(1)}, u32[]{:S(2)}, u32[]{:S(2)}) collective-permute-start(f32[16,128]{1,0:T(8,128)S(1)} %get-tuple-element.43), channel_id=1, source_target_pairs={{0,240},{1,241},{2,242},{3,243},{4,244},{5,245},{6,246},{7,247},{8... | collective-permute-start | bytes 24584 | tf_op jit(solution)/shard_map/ppermute | solution.py:652
  22.1 0.2 seam_own.1.refs_2_
  22.3 2.0 %border_rows.1 = (f32[4,4,8,8,128]{4,3,2,1,0:T(8,128)}, f32[4,4,8,8,128]{4,3,2,1,0:T(8,128)}, f32[4,4,8,8,128]{4,3,2,1,0:T(8,128)}, f32[4,4,8,8,128]{4,3,2,1,0:T(8,128)}, f32[4,4,8,8,128]{4,3,2,1,0:T(8,128)}) custom-call(f32[352,128]{1,0:T(8,128)S(1)} %collective-permute-done.recv_a.re, ...), custom_call_target="tpu_custom_call", output_to_operand_aliasing={{0}: (3, {}), {1}: (4, {}), {2}: (5, {}), {3}: (6, {}), {4}... | custom-call | flops 4194304 | bytes 4194304 | tf_op jit(solution)/shard_map/border_rows/pallas_call | solution.py:655
  24.3 0.0 collective-permute-done.2.refs_0_
  24.4 1.0 %collective-permute-done.3.refs_1_ = f32[16,128]{1,0:T(8,128)S(1)} collective-permute-done((f32[16,128]{1,0:T(8,128)S(1)}, f32[16,128]{1,0:T(8,128)S(1)}, u32[]{:S(2)}, u32[]{:S(2)}) %collective-permute-start.3) | collective-permute-done | bytes 8224 | tf_op jit(solution)/shard_map/ppermute | solution.py:652
  25.3 2.7 %seam_columns.1 = (f32[4,4,64,128]{3,2,1,0:T(8,128)}, f32[4,4,64,128]{3,2,1,0:T(8,128)}, f32[4,4,64,128]{3,2,1,0:T(8,128)}, f32[4,4,64,128]{3,2,1,0:T(8,128)}, f32[4,4,64,128]{3,2,1,0:T(8,128)}) custom-call(f32[16,128]{1,0:T(8,128)S(1)} %collective-permute-done.2.refs_0_, ...), custom_call_target="tpu_custom_call", output_to_operand_aliasing={{0}: (3, {}), {1}: (4, {}), {2}: (5, {}), {3}: (6, {}), {4}... | custom-call | tf_op jit(solution)/shard_map/seam_columns/pallas_call | solution.py:682
Async XLA Ops:
  3.3 12.6 %collective-permute-start = (f32[352,128]{1,0:T(8,128)S(1)}, f32[352,128]{1,0:T(8,128)S(1)}, u32[]{:S(2)}, u32[]{:S(2)}) collective-permute-start(f32[352,128]{1,0:T(8,128)S(1)} %get-tuple-element.33), channel_id=1, source_target_pairs={{0,1},{1,0},{2,3},{3,2},{4,5},{5,4},{6,7},{7,6},{8,9},{9,8},{10,11... | collective-permute-start | bytes 540680 | tf_op jit(solution)/shard_map/ppermute | solution.py:640
  3.7 14.7 %collective-permute-start.1 = (f32[352,128]{1,0:T(8,128)S(1)}, f32[352,128]{1,0:T(8,128)S(1)}, u32[]{:S(2)}, u32[]{:S(2)}) collective-permute-start(f32[352,128]{1,0:T(8,128)S(1)} %get-tuple-element.34), channel_id=1, source_target_pairs={{1,2},{2,1},{3,4},{4,3},{5,6},{6,5},{7,8},{8,7},{9,10},{10,9},{11,... | collective-permute-start | bytes 540680 | tf_op jit(solution)/shard_map/ppermute | solution.py:639
  18.6 5.8 %collective-permute-start.2 = (f32[16,128]{1,0:T(8,128)S(1)}, f32[16,128]{1,0:T(8,128)S(1)}, u32[]{:S(2)}, u32[]{:S(2)}) collective-permute-start(f32[16,128]{1,0:T(8,128)S(1)} %get-tuple-element.42), channel_id=1, source_target_pairs={{0,16},{1,17},{2,18},{3,19},{4,20},{5,21},{6,22},{7,23},{8,24},{9,... | collective-permute-start | bytes 24584 | tf_op jit(solution)/shard_map/ppermute | solution.py:653
  18.6 6.8 %collective-permute-start.3 = (f32[16,128]{1,0:T(8,128)S(1)}, f32[16,128]{1,0:T(8,128)S(1)}, u32[]{:S(2)}, u32[]{:S(2)}) collective-permute-start(f32[16,128]{1,0:T(8,128)S(1)} %get-tuple-element.43), channel_id=1, source_target_pairs={{0,240},{1,241},{2,242},{3,243},{4,244},{5,245},{6,246},{7,247},{8... | collective-permute-start | bytes 24584 | tf_op jit(solution)/shard_map/ppermute | solution.py:652

commit v3 on v2

--- a/solution.py
+++ b/solution.py
@@ -17,7 +17,8 @@
 
 LEVELS = 4
 UNROLL = 8
-LIMIT = 50.3
+LIMIT = 53.4
+LIMIT_BRING = 50.0
 FIELDS = 5
 ROWS = 32
 COLS = 1024
@@ -139,23 +140,19 @@
 
 def rows_kernel(*refs):
     args = refs[:6]
-    msg_a, msg_b = refs[6:8]
-    kept = refs[8:14]
-    scratch, sems = refs[14:]
-    copies = [
-        [
-            pltpu.make_async_copy(args[f].at[:, t], kept[f].at[:, t], sems.at[t, f])
-            for f in range(6)
-        ]
-        for t in range(4)
-    ]
-    for t in (0, 3, 1, 2):
-        for copy in copies[t]:
-            copy.start()
-    for t in (0, 3):
-        for copy in copies[t]:
-            copy.wait()
-    low, high = ([x.at[:, t] for x in kept] for t in (0, 3))
+    msg_a, msg_b, scratch, floats, ints, sems = refs[6:]
+    low, high, copies = [], [], []
+    for side, rows in enumerate((low, high)):
+        for f in range(6):
+            here = floats.at[side, f] if f < FIELDS else ints.at[side]
+            rows.append(here)
+            two = pl.ds(6 * side, 2)
+            tile = args[f].at[:, 3 * side, :, two, :]
+            copies.append(pltpu.make_async_copy(tile, here.at[:, :, two, :], sems.at[side, f]))
+    for copy in copies:
+        copy.start()
+    for copy in copies:
+        copy.wait()
     lat = lax.axis_index("lat")
     last = lax.axis_size("lat") - 1
     odd = lax.rem(lat, 2) == 1
@@ -194,9 +191,18 @@
         for s in range(8):
             msg_b[pl.ds(7 - s, PLANES, stride=8), :] = scratch[pl.ds(s, PLANES, stride=8), :]
 
-    for t in (1, 2):
-        for copy in copies[t]:
-            copy.wait()
+
+def bring_kernel(*refs):
+    args, kept, sems = refs[:6], refs[6:12], refs[12]
+    copies = [
+        pltpu.make_async_copy(args[f].at[:, t], kept[f].at[:, t], sems.at[f, t])
+        for f in range(6)
+        for t in range(4)
+    ]
+    for copy in copies:
+        copy.start()
+    for copy in copies:
+        copy.wait()
 
 
 def inner_kernel(*refs):
@@ -462,9 +468,9 @@
 
 
 def seam_kernel(*refs):
-    recv_a, recv_b, own = refs[:3]
+    recv_b, recv_a, own = refs[:3]
     outs = refs[8:13]
-    left, right, sems = refs[13:]
+    left, right, turned, sems = refs[13:]
     loads = []
     for f in range(FIELDS):
         loads.append(pltpu.make_async_copy(outs[f].at[:, :, pl.ds(0, 8), :], left.at[f], sems.at[f]))
@@ -486,8 +492,8 @@
     from_east = [pltpu.roll(jnp.where(lon_odd, b, a), 64, 1) for a, b in zip(pa, pb)]
 
     w_s, w_n = pltpu.roll(from_west[1], 5, 0), pltpu.roll(from_west[1], 4, 0)
-    turned = pltpu.roll(from_east[1], 64, 1)
-    e_s, e_n = pltpu.roll(turned, 2, 0), pltpu.roll(turned, 1, 0)
+    back = pltpu.roll(from_east[1], 64, 1)
+    e_s, e_n = pltpu.roll(back, 2, 0), pltpu.roll(back, 1, 0)
     corner = spots(w_s, w_n, e_s, e_n)
     at_corner = jnp.logical_and(at_spot(lane), sub == jnp.where(lane < 64, 1, 6))
     row = lax.rem(lane, 64) - 1
@@ -531,8 +537,6 @@
                 new_q[i] = new[f] + brought[i] if s == 0 else new[f]
         q = new_q
 
-    for copy in loads:
-        copy.wait()
     big_lane = iota(1, (128, 128))
     gap = jnp.zeros((112, 128), jnp.float32)
     for f in range(FIELDS):
@@ -543,11 +547,14 @@
             w = jnp.where(here, pltpu.roll(x, (32 * k - 1) % 128, 1), w)
             e = jnp.where(here, pltpu.roll(x, (32 * k - 65) % 128, 1), e)
         w, e = pltpu.roll(w, 6, 0), pltpu.roll(e, 2, 0)
-        turned = jnp.concatenate([w, gap, e], axis=0).T
+        turned[f] = jnp.concatenate([w, gap, e], axis=0).T
+    for copy in loads:
+        copy.wait()
+    for f in range(FIELDS):
         a = left[f].reshape(128, 128)
         b = right[f].reshape(128, 128)
-        left[f] = jnp.where(big_lane < 2, turned, a).reshape(LEVELS, 4, 8, 128)
-        right[f] = jnp.where(big_lane >= 126, turned, b).reshape(LEVELS, 4, 8, 128)
+        left[f] = jnp.where(big_lane < 2, turned[f], a).reshape(LEVELS, 4, 8, 128)
+        right[f] = jnp.where(big_lane >= 126, turned[f], b).reshape(LEVELS, 4, 8, 128)
     stores = []
     for f in range(FIELDS):
         stores.append(pltpu.make_async_copy(left.at[f], outs[f].at[:, :, pl.ds(0, 8), :], sems.at[f]))
@@ -621,15 +628,16 @@
     planes = EDGE_PLANES
 
     split = (LEVELS, 4, 8, 8, 128)
-    kept = [jax.ShapeDtypeStruct(split, x.dtype) for x in args]
-    send_a, send_b, *args = pl.pallas_call(
+    send_a, send_b = pl.pallas_call(
         rows_kernel,
         in_specs=[HBM] * 6,
-        out_specs=[VMEM] * 8,
-        out_shape=[f32(PLANES * 8, 128)] * 2 + kept,
+        out_specs=[VMEM] * 2,
+        out_shape=[f32(PLANES * 8, 128)] * 2,
         scratch_shapes=[
             pltpu.VMEM((PLANES * 8, 128), jnp.float32),
-            pltpu.SemaphoreType.DMA((4, 6)),
+            pltpu.VMEM((2, FIELDS, LEVELS, 8, 8, 128), jnp.float32),
+            pltpu.VMEM((2, LEVELS, 8, 8, 128), jnp.int32),
+            pltpu.SemaphoreType.DMA((2, 6)),
         ],
         compiler_params=params(LIMIT),
         cost_estimate=pl.CostEstimate(flops=1 << 20, bytes_accessed=2 << 20, transcendentals=0),
@@ -639,6 +647,16 @@
     recv_b = lax.ppermute(send_b, axes, lat_b)
     recv_a = lax.ppermute(send_a, axes, lat_a)
 
+    args = pl.pallas_call(
+        bring_kernel,
+        in_specs=[HBM] * 6,
+        out_specs=[VMEM] * 6,
+        out_shape=[jax.ShapeDtypeStruct(x.shape, x.dtype) for x in args],
+        scratch_shapes=[pltpu.SemaphoreType.DMA((6, 4))],
+        compiler_params=params(LIMIT_BRING),
+        cost_estimate=pl.CostEstimate(flops=0, bytes_accessed=6 << 20, transcendentals=0),
+        name="bring_fields",
+    )(*args)
     *inner, edge, cols = inner_call(args)
 
     send_la, send_lb, halos = pl.pallas_call(
@@ -688,11 +706,12 @@
         scratch_shapes=[
             pltpu.VMEM((FIELDS, LEVELS, 4, 8, 128), jnp.float32),
             pltpu.VMEM((FIELDS, LEVELS, 4, 8, 128), jnp.float32),
+            pltpu.VMEM((FIELDS, 128, 128), jnp.float32),
             pltpu.SemaphoreType.DMA((2 * FIELDS,)),
         ],
         compiler_params=params(16),
         name="seam_columns",
-    )(recv_la, recv_lb, own, *(x.reshape(LEVELS, 4, 64, 128) for x in border))
+    )(recv_lb, recv_la, own, *(x.reshape(LEVELS, 4, 64, 128) for x in border))
     return tuple(unview(x) for x in final)
 
 

time: 28.2 us -> 27.5 us (0.975)
  the two profiles are of different devices: /device:TPU:232 before, /device:TPU:104 now
where the time goes in v3:
time: 27.5 us; the launch traced here: 27.2 us
  Pallas kernels  15.4 us (56%)
  starting transfers between devices  9.96 us (36%)
  waiting for transfers between devices  1.09 us (4%)
  between operations  0.71 us (3%)
    pallas_call x1, Pallas kernels, inner_call(): pl.pallas_call(inner_kernel, in_specs=[VMEM] * 6, out_specs=[HBM] * FIELD...  6.37 us
    ppermute x1, starting transfers between devices, per_device(): recv_b = lax.ppermute(send_b, axes, lat_b)  6.04 us
    ppermute x1, starting transfers between devices, per_device(): recv_lb = lax.ppermute(send_lb, axes, lon_b)  3.38 us
    pallas_call x1, Pallas kernels, per_device(): pl.pallas_call(seam_kernel, in_specs=[VMEM] * 3 + [HBM] * FIELDS, out_spe...  2.67 us
    pallas_call x1, Pallas kernels, per_device(): pl.pallas_call(bring_kernel, in_specs=[HBM] * 6, out_specs=[VMEM] * 6, ou...  2.15 us
    pallas_call x1, Pallas kernels, per_device(): pl.pallas_call(border_kernel, in_specs=[VMEM] * 2 + [HBM] * (1 + FIELDS),...  2 us
    pallas_call x1, Pallas kernels, per_device(): pl.pallas_call(rows_kernel, in_specs=[HBM] * 6, out_specs=[VMEM] * 2, out...  1.82 us
    ppermute x1, waiting for transfers between devices, per_device(): recv_lb = lax.ppermute(send_lb, axes, lon_b)  1.08 us
  transfers between devices with their start and end apart: 4, of which 1 were waited for; matrix products, arithmetic and copies ran while one was open for 0% of the time, Pallas kernels for 39%

profile of v3, /device:TPU:104, one launch (start us, length us, event | category | flops | bytes accessed | tf_op | source)
XLA Modules:
  0.0 27.2 jit_solution(4228229729389520922)
XLA Ops:
  0.6 0.0 copy-start
  0.6 1.8 %edge_rows.1 = (f32[352,128]{1,0:T(8,128)S(1)}, f32[352,128]{1,0:T(8,128)S(1)}) custom-call(f32[4,4,8,8,128]{4,3,2,1,0:T(8,128)} %bitcast.65, f32[4,4,8,8,128]{4,3,2,1,0:T(8,128)} %bitcast.82, f32[4,4,8,8,128]{4,3,2,1,0:T(8,128)} %bitcast.84, f32[4,4,8,8,128]{4,3,2,1,0:T(8,128)} %bitcast.86, f32[4,4,8,8,128]{4,3,2,1,0:T(8,128)} %bitcast.88, ...), custom_call_target="tpu_custom_call" | custom-call | flops 1048576 | bytes 2097152 | tf_op jit(solution)/shard_map/edge_rows/pallas_call | solution.py:631
  2.5 0.5 %collective-permute-start = (f32[352,128]{1,0:T(8,128)S(1)}, f32[352,128]{1,0:T(8,128)S(1)}, u32[]{:S(2)}, u32[]{:S(2)}) collective-permute-start(f32[352,128]{1,0:T(8,128)S(1)} %get-tuple-element.33), channel_id=1, source_target_pairs={{0,1},{1,0},{2,3},{3,2},{4,5},{5,4},{6,7},{7,6},{8,9},{9,8},{10,11... | collective-permute-start | bytes 540680 | tf_op jit(solution)/shard_map/ppermute | solution.py:648
  3.0 6.0 %collective-permute-start.1 = (f32[352,128]{1,0:T(8,128)S(1)}, f32[352,128]{1,0:T(8,128)S(1)}, u32[]{:S(2)}, u32[]{:S(2)}) collective-permute-start(f32[352,128]{1,0:T(8,128)S(1)} %get-tuple-element.34), channel_id=1, source_target_pairs={{1,2},{2,1},{3,4},{4,3},{5,6},{6,5},{7,8},{8,7},{9,10},{10,9},{11,... | collective-permute-start | bytes 540680 | tf_op jit(solution)/shard_map/ppermute | solution.py:647
  9.1 0.0 copy-done
  9.1 2.1 %bring_fields.1 = (f32[4,4,64,128]{3,2,1,0:T(8,128)S(1)}, f32[4,4,64,128]{3,2,1,0:T(8,128)S(1)}, f32[4,4,64,128]{3,2,1,0:T(8,128)S(1)}, f32[4,4,64,128]{3,2,1,0:...) custom-call(f32[4,4,64,128]{3,2,1,0:T(8,128)S(1)} %bitcast.66, f32[4,4,64,128]{3,2,1,0:T(8,128)} %bitcast.83, ...), custom_call_target="tpu_custom_call" | custom-call | bytes 6291456 | tf_op jit(solution)/shard_map/bring_fields/pallas_call | solution.py:650
  11.2 6.4 %inner_rows.1 = (f32[4,4,64,128]{3,2,1,0:T(8,128)}, f32[4,4,64,128]{3,2,1,0:T(8,128)}, f32[4,4,64,128]{3,2,1,0:T(8,128)}, f32[4,4,64,128]{3,2,1,0:T(8,128)}, f32...) custom-call(f32[4,4,64,128]{3,2,1,0:T(8,128)S(1)} %get-tuple-element.35.refs_0_, ...), custom_call_target="tpu_custom_call" | custom-call | flops 27262976 | bytes 6291456 | tf_op jit(solution)/shard_map/inner_rows/pallas_call | solution.py:602
  17.6 0.0 collective-permute-done.recv_a.refs_0_
  17.6 0.0 collective-permute-done.1.recv_b.refs_1_
  17.6 0.2 edge_columns.1
  17.8 3.4 %collective-permute-start.2 = (f32[16,128]{1,0:T(8,128)S(1)}, f32[16,128]{1,0:T(8,128)S(1)}, u32[]{:S(2)}, u32[]{:S(2)}) collective-permute-start(f32[16,128]{1,0:T(8,128)S(1)} %get-tuple-element.42), channel_id=1, source_target_pairs={{0,240},{1,241},{2,242},{3,243},{4,244},{5,245},{6,246},{7,247},{8... | collective-permute-start | bytes 24584 | tf_op jit(solution)/shard_map/ppermute | solution.py:670
  21.2 0.0 collective-permute-start.3
  21.2 0.2 seam_own.1.refs_2_
  21.4 2.0 %border_rows.1 = (f32[4,4,8,8,128]{4,3,2,1,0:T(8,128)}, f32[4,4,8,8,128]{4,3,2,1,0:T(8,128)}, f32[4,4,8,8,128]{4,3,2,1,0:T(8,128)}, f32[4,4,8,8,128]{4,3,2,1,0:T(8,128)}, f32[4,4,8,8,128]{4,3,2,1,0:T(8,128)}) custom-call(f32[352,128]{1,0:T(8,128)S(1)} %collective-permute-done.recv_a.re, ...), custom_call_target="tpu_custom_call", output_to_operand_aliasing={{0}: (3, {}), {1}: (4, {}), {2}: (5, {}), {3}: (6, {}), {4}... | custom-call | flops 4194304 | bytes 4194304 | tf_op jit(solution)/shard_map/border_rows/pallas_call | solution.py:673
  23.4 1.1 %collective-permute-done.2.refs_0_ = f32[16,128]{1,0:T(8,128)S(1)} collective-permute-done((f32[16,128]{1,0:T(8,128)S(1)}, f32[16,128]{1,0:T(8,128)S(1)}, u32[]{:S(2)}, u32[]{:S(2)}) %collective-permute-start.2) | collective-permute-done | bytes 8224 | tf_op jit(solution)/shard_map/ppermute | solution.py:670
  24.5 0.0 collective-permute-done.3.refs_1_
  24.5 2.7 %seam_columns.1 = (f32[4,4,64,128]{3,2,1,0:T(8,128)}, f32[4,4,64,128]{3,2,1,0:T(8,128)}, f32[4,4,64,128]{3,2,1,0:T(8,128)}, f32[4,4,64,128]{3,2,1,0:T(8,128)}, f32[4,4,64,128]{3,2,1,0:T(8,128)}) custom-call(f32[16,128]{1,0:T(8,128)S(1)} %collective-permute-done.2.refs_0_, ...), custom_call_target="tpu_custom_call", output_to_operand_aliasing={{0}: (3, {}), {1}: (4, {}), {2}: (5, {}), {3}: (6, {}), {4}... | custom-call | tf_op jit(solution)/shard_map/seam_columns/pallas_call | solution.py:700
Async XLA Ops:
  0.6 8.4 %copy-start = (f32[4,32,1024]{2,1,0:T(8,128)S(1)}, f32[4,32,1024]{2,1,0:T(8,128)}, u32[]{:S(2)}) copy-start(f32[4,32,1024]{2,1,0:T(8,128)} %param.6) | copy-start | bytes 1572868
  2.5 15.1 %collective-permute-start = (f32[352,128]{1,0:T(8,128)S(1)}, f32[352,128]{1,0:T(8,128)S(1)}, u32[]{:S(2)}, u32[]{:S(2)}) collective-permute-start(f32[352,128]{1,0:T(8,128)S(1)} %get-tuple-element.33), channel_id=1, source_target_pairs={{0,1},{1,0},{2,3},{3,2},{4,5},{5,4},{6,7},{7,6},{8,9},{9,8},{10,11... | collective-permute-start | bytes 540680 | tf_op jit(solution)/shard_map/ppermute | solution.py:648
  3.0 14.6 %collective-permute-start.1 = (f32[352,128]{1,0:T(8,128)S(1)}, f32[352,128]{1,0:T(8,128)S(1)}, u32[]{:S(2)}, u32[]{:S(2)}) collective-permute-start(f32[352,128]{1,0:T(8,128)S(1)} %get-tuple-element.34), channel_id=1, source_target_pairs={{1,2},{2,1},{3,4},{4,3},{5,6},{6,5},{7,8},{8,7},{9,10},{10,9},{11,... | collective-permute-start | bytes 540680 | tf_op jit(solution)/shard_map/ppermute | solution.py:647
  17.8 6.7 %collective-permute-start.2 = (f32[16,128]{1,0:T(8,128)S(1)}, f32[16,128]{1,0:T(8,128)S(1)}, u32[]{:S(2)}, u32[]{:S(2)}) collective-permute-start(f32[16,128]{1,0:T(8,128)S(1)} %get-tuple-element.42), channel_id=1, source_target_pairs={{0,240},{1,241},{2,242},{3,243},{4,244},{5,245},{6,246},{7,247},{8... | collective-permute-start | bytes 24584 | tf_op jit(solution)/shard_map/ppermute | solution.py:670
  21.2 3.3 %collective-permute-start.3 = (f32[16,128]{1,0:T(8,128)S(1)}, f32[16,128]{1,0:T(8,128)S(1)}, u32[]{:S(2)}, u32[]{:S(2)}) collective-permute-start(f32[16,128]{1,0:T(8,128)S(1)} %get-tuple-element.43), channel_id=1, source_target_pairs={{0,16},{1,17},{2,18},{3,19},{4,20},{5,21},{6,22},{7,23},{8,24},{9,... | collective-permute-start | bytes 24584 | tf_op jit(solution)/shard_map/ppermute | solution.py:671

commit v4 on v3

--- a/solution.py
+++ b/solution.py
@@ -195,9 +195,7 @@
 def bring_kernel(*refs):
     args, kept, sems = refs[:6], refs[6:12], refs[12]
     copies = [
-        pltpu.make_async_copy(args[f].at[:, t], kept[f].at[:, t], sems.at[f, t])
-        for f in range(6)
-        for t in range(4)
+        pltpu.make_async_copy(args[f], kept[f], sems.at[f, 0]) for f in range(6)
     ]
     for copy in copies:
         copy.start()
@@ -550,21 +548,20 @@
         turned[f] = jnp.concatenate([w, gap, e], axis=0).T
     for copy in loads:
         copy.wait()
+    stores = []
     for f in range(FIELDS):
         a = left[f].reshape(128, 128)
         b = right[f].reshape(128, 128)
         left[f] = jnp.where(big_lane < 2, turned[f], a).reshape(LEVELS, 4, 8, 128)
         right[f] = jnp.where(big_lane >= 126, turned[f], b).reshape(LEVELS, 4, 8, 128)
-    stores = []
-    for f in range(FIELDS):
         stores.append(pltpu.make_async_copy(left.at[f], outs[f].at[:, :, pl.ds(0, 8), :], sems.at[f]))
         stores.append(
             pltpu.make_async_copy(
                 right.at[f], outs[f].at[:, :, pl.ds(56, 8), :], sems.at[FIELDS + f]
             )
         )
-    for copy in stores:
-        copy.start()
+        stores[-2].start()
+        stores[-1].start()
     for copy in stores:
         copy.wait()
 

time: 27.5 us -> 27.4 us (level)
  no operation moved by 1% of the time
where the time goes in v4:
time: 27.4 us; the launch traced here: 26.9 us
  Pallas kernels  15.2 us (55%)
  starting transfers between devices  9.96 us (36%)
  waiting for transfers between devices  1.09 us (4%)
  between operations  0.71 us (3%)
    pallas_call x1, Pallas kernels, inner_call(): pl.pallas_call(inner_kernel, in_specs=[VMEM] * 6, out_specs=[HBM] * FIELD...  6.37 us
    ppermute x1, starting transfers between devices, per_device(): recv_b = lax.ppermute(send_b, axes, lat_b)  6.04 us
    ppermute x1, starting transfers between devices, per_device(): recv_lb = lax.ppermute(send_lb, axes, lon_b)  3.38 us
    pallas_call x1, Pallas kernels, per_device(): pl.pallas_call(seam_kernel, in_specs=[VMEM] * 3 + [HBM] * FIELDS, out_spe...  2.64 us
    pallas_call x1, Pallas kernels, per_device(): pl.pallas_call(border_kernel, in_specs=[VMEM] * 2 + [HBM] * (1 + FIELDS),...  2 us
    pallas_call x1, Pallas kernels, per_device(): pl.pallas_call(bring_kernel, in_specs=[HBM] * 6, out_specs=[VMEM] * 6, ou...  1.93 us
    pallas_call x1, Pallas kernels, per_device(): pl.pallas_call(rows_kernel, in_specs=[HBM] * 6, out_specs=[VMEM] * 2, out...  1.82 us
    ppermute x1, waiting for transfers between devices, per_device(): recv_lb = lax.ppermute(send_lb, axes, lon_b)  1.08 us
  transfers between devices with their start and end apart: 4, of which 1 were waited for; matrix products, arithmetic and copies ran while one was open for 0% of the time, Pallas kernels for 39%

profile of v4, /device:TPU:104, one launch (start us, length us, event | category | flops | bytes accessed | tf_op | source)
XLA Modules:
  0.0 26.9 jit_solution(15771301415232410345)
XLA Ops:
  0.6 0.0 copy-start
  0.6 1.8 %edge_rows.1 = (f32[352,128]{1,0:T(8,128)S(1)}, f32[352,128]{1,0:T(8,128)S(1)}) custom-call(f32[4,4,8,8,128]{4,3,2,1,0:T(8,128)} %bitcast.65, f32[4,4,8,8,128]{4,3,2,1,0:T(8,128)} %bitcast.82, f32[4,4,8,8,128]{4,3,2,1,0:T(8,128)} %bitcast.84, f32[4,4,8,8,128]{4,3,2,1,0:T(8,128)} %bitcast.86, f32[4,4,8,8,128]{4,3,2,1,0:T(8,128)} %bitcast.88, ...), custom_call_target="tpu_custom_call" | custom-call | flops 1048576 | bytes 2097152 | tf_op jit(solution)/shard_map/edge_rows/pallas_call | solution.py:628
  2.5 0.5 %collective-permute-start = (f32[352,128]{1,0:T(8,128)S(1)}, f32[352,128]{1,0:T(8,128)S(1)}, u32[]{:S(2)}, u32[]{:S(2)}) collective-permute-start(f32[352,128]{1,0:T(8,128)S(1)} %get-tuple-element.33), channel_id=1, source_target_pairs={{0,1},{1,0},{2,3},{3,2},{4,5},{5,4},{6,7},{7,6},{8,9},{9,8},{10,11... | collective-permute-start | bytes 540680 | tf_op jit(solution)/shard_map/ppermute | solution.py:645
  3.0 6.0 %collective-permute-start.1 = (f32[352,128]{1,0:T(8,128)S(1)}, f32[352,128]{1,0:T(8,128)S(1)}, u32[]{:S(2)}, u32[]{:S(2)}) collective-permute-start(f32[352,128]{1,0:T(8,128)S(1)} %get-tuple-element.34), channel_id=1, source_target_pairs={{1,2},{2,1},{3,4},{4,3},{5,6},{6,5},{7,8},{8,7},{9,10},{10,9},{11,... | collective-permute-start | bytes 540680 | tf_op jit(solution)/shard_map/ppermute | solution.py:644
  9.1 0.0 copy-done
  9.1 1.9 %bring_fields.1 = (f32[4,4,64,128]{3,2,1,0:T(8,128)S(1)}, f32[4,4,64,128]{3,2,1,0:T(8,128)S(1)}, f32[4,4,64,128]{3,2,1,0:T(8,128)S(1)}, f32[4,4,64,128]{3,2,1,0:...) custom-call(f32[4,4,64,128]{3,2,1,0:T(8,128)S(1)} %bitcast.66, f32[4,4,64,128]{3,2,1,0:T(8,128)} %bitcast.83, ...), custom_call_target="tpu_custom_call" | custom-call | bytes 6291456 | tf_op jit(solution)/shard_map/bring_fields/pallas_call | solution.py:647
  11.0 6.4 %inner_rows.1 = (f32[4,4,64,128]{3,2,1,0:T(8,128)}, f32[4,4,64,128]{3,2,1,0:T(8,128)}, f32[4,4,64,128]{3,2,1,0:T(8,128)}, f32[4,4,64,128]{3,2,1,0:T(8,128)}, f32...) custom-call(f32[4,4,64,128]{3,2,1,0:T(8,128)S(1)} %get-tuple-element.35.refs_0_, ...), custom_call_target="tpu_custom_call" | custom-call | flops 27262976 | bytes 6291456 | tf_op jit(solution)/shard_map/inner_rows/pallas_call | solution.py:599
  17.4 0.0 collective-permute-done.recv_a.refs_0_
  17.4 0.0 collective-permute-done.1.recv_b.refs_1_
  17.4 0.2 edge_columns.1
  17.6 3.4 %collective-permute-start.2 = (f32[16,128]{1,0:T(8,128)S(1)}, f32[16,128]{1,0:T(8,128)S(1)}, u32[]{:S(2)}, u32[]{:S(2)}) collective-permute-start(f32[16,128]{1,0:T(8,128)S(1)} %get-tuple-element.42), channel_id=1, source_target_pairs={{0,240},{1,241},{2,242},{3,243},{4,244},{5,245},{6,246},{7,247},{8... | collective-permute-start | bytes 24584 | tf_op jit(solution)/shard_map/ppermute | solution.py:667
  21.0 0.0 collective-permute-start.3
  21.0 0.2 seam_own.1.refs_2_
  21.2 2.0 %border_rows.1 = (f32[4,4,8,8,128]{4,3,2,1,0:T(8,128)}, f32[4,4,8,8,128]{4,3,2,1,0:T(8,128)}, f32[4,4,8,8,128]{4,3,2,1,0:T(8,128)}, f32[4,4,8,8,128]{4,3,2,1,0:T(8,128)}, f32[4,4,8,8,128]{4,3,2,1,0:T(8,128)}) custom-call(f32[352,128]{1,0:T(8,128)S(1)} %collective-permute-done.recv_a.re, ...), custom_call_target="tpu_custom_call", output_to_operand_aliasing={{0}: (3, {}), {1}: (4, {}), {2}: (5, {}), {3}: (6, {}), {4}... | custom-call | flops 4194304 | bytes 4194304 | tf_op jit(solution)/shard_map/border_rows/pallas_call | solution.py:670
  23.2 1.1 %collective-permute-done.2.refs_0_ = f32[16,128]{1,0:T(8,128)S(1)} collective-permute-done((f32[16,128]{1,0:T(8,128)S(1)}, f32[16,128]{1,0:T(8,128)S(1)}, u32[]{:S(2)}, u32[]{:S(2)}) %collective-permute-start.2) | collective-permute-done | bytes 8224 | tf_op jit(solution)/shard_map/ppermute | solution.py:667
  24.3 0.0 collective-permute-done.3.refs_1_
  24.3 2.6 %seam_columns.1 = (f32[4,4,64,128]{3,2,1,0:T(8,128)}, f32[4,4,64,128]{3,2,1,0:T(8,128)}, f32[4,4,64,128]{3,2,1,0:T(8,128)}, f32[4,4,64,128]{3,2,1,0:T(8,128)}, f32[4,4,64,128]{3,2,1,0:T(8,128)}) custom-call(f32[16,128]{1,0:T(8,128)S(1)} %collective-permute-done.2.refs_0_, ...), custom_call_target="tpu_custom_call", output_to_operand_aliasing={{0}: (3, {}), {1}: (4, {}), {2}: (5, {}), {3}: (6, {}), {4}... | custom-call | tf_op jit(solution)/shard_map/seam_columns/pallas_call | solution.py:697
Async XLA Ops:
  0.6 8.4 %copy-start = (f32[4,32,1024]{2,1,0:T(8,128)S(1)}, f32[4,32,1024]{2,1,0:T(8,128)}, u32[]{:S(2)}) copy-start(f32[4,32,1024]{2,1,0:T(8,128)} %param.6) | copy-start | bytes 1572868
  2.5 14.9 %collective-permute-start = (f32[352,128]{1,0:T(8,128)S(1)}, f32[352,128]{1,0:T(8,128)S(1)}, u32[]{:S(2)}, u32[]{:S(2)}) collective-permute-start(f32[352,128]{1,0:T(8,128)S(1)} %get-tuple-element.33), channel_id=1, source_target_pairs={{0,1},{1,0},{2,3},{3,2},{4,5},{5,4},{6,7},{7,6},{8,9},{9,8},{10,11... | collective-permute-start | bytes 540680 | tf_op jit(solution)/shard_map/ppermute | solution.py:645
  3.0 14.4 %collective-permute-start.1 = (f32[352,128]{1,0:T(8,128)S(1)}, f32[352,128]{1,0:T(8,128)S(1)}, u32[]{:S(2)}, u32[]{:S(2)}) collective-permute-start(f32[352,128]{1,0:T(8,128)S(1)} %get-tuple-element.34), channel_id=1, source_target_pairs={{1,2},{2,1},{3,4},{4,3},{5,6},{6,5},{7,8},{8,7},{9,10},{10,9},{11,... | collective-permute-start | bytes 540680 | tf_op jit(solution)/shard_map/ppermute | solution.py:644
  17.6 6.7 %collective-permute-start.2 = (f32[16,128]{1,0:T(8,128)S(1)}, f32[16,128]{1,0:T(8,128)S(1)}, u32[]{:S(2)}, u32[]{:S(2)}) collective-permute-start(f32[16,128]{1,0:T(8,128)S(1)} %get-tuple-element.42), channel_id=1, source_target_pairs={{0,240},{1,241},{2,242},{3,243},{4,244},{5,245},{6,246},{7,247},{8... | collective-permute-start | bytes 24584 | tf_op jit(solution)/shard_map/ppermute | solution.py:667
  21.0 3.3 %collective-permute-start.3 = (f32[16,128]{1,0:T(8,128)S(1)}, f32[16,128]{1,0:T(8,128)S(1)}, u32[]{:S(2)}, u32[]{:S(2)}) collective-permute-start(f32[16,128]{1,0:T(8,128)S(1)} %get-tuple-element.43), channel_id=1, source_target_pairs={{0,16},{1,17},{2,18},{3,19},{4,20},{5,21},{6,22},{7,23},{8,24},{9,... | collective-permute-start | bytes 24584 | tf_op jit(solution)/shard_map/ppermute | solution.py:668
